TPU v7x, 512 devices: a whole 4x8x8 slice. The times are simulated.
512 devices in a mesh: space: 32 (over x, z_hi, core), sect: 16 (over z_lo, y).
Axes of the slice: x: 4, y: 8, z: 8 (z_hi: 4, z_lo: 2; z = z_hi * 2 + z_lo), core: 2. Of those that a mesh axis runs over, the one named last changes fastest.
Arguments:
- density: float32 [96, 128, 2048], P('space', 'sect'), may hold values from 0.05 to 1
- velocity: float32 [96, 2048], P('space'), may hold values from -0.9 to 0.9
- kernel: float32 [128, 128], replicated, may hold values from 0.00078125 to 0.0078125
- split: float32 [128, 128], replicated, may hold values from 0 to 1
- target: int32 [128, 128], replicated, may hold values from 0 to 126, as said below
Outputs:
- updated: float32 [96, 128, 2048], P('space', 'sect')
Inputs may be any that keep to these rules, and one draw needn't show every extreme that they name: target is symmetric, and target[i][j] is at least min(max(i, j), 126).
All inputs are finite; a program needn't handle non-finite values.
Results may differ from a plain program's by a relative error of at most 0.00058.
Values may be sent and summed in bfloat16 or wider, within the bound.
No kernel may reach another device: no remote copies, remote signals or barrier semaphores. Data moves between devices by JAX's collectives and lax.ppermute only.
A program may use at most 64 MiB of HBM per device.

v0:
```python
import jax
import jax.numpy as jnp
from jax import lax
from jax.experimental import pallas as pl
from jax.experimental.pallas import tpu as pltpu
from jax.sharding import Mesh
from jax.sharding import PartitionSpec as P

K = 128
CELLS = 128
BLOCKS = 8
B = 16
SECT = ("zl", "y")
SPACE = ("chip", "core")
VMEM = pl.BlockSpec(memory_space=pltpu.VMEM)
SMEM = pl.BlockSpec(memory_space=pltpu.SMEM)
F32 = jnp.float32
BF16 = jnp.bfloat16


def params(mib):
    return pltpu.CompilerParams(vmem_limit_bytes=mib * 1024 * 1024)


def prepare_kernel(kernel_ref, split_ref, target_ref, beta_ref, *coef_refs):
    kernel, split = kernel_ref[...], split_ref[...]
    beta = 0.5 * (kernel + kernel.T)
    weight = 0.5 * (split + split.T)
    beta_ref[...] = beta.astype(BF16)
    rows = lax.broadcasted_iota(jnp.int32, (K, K), 0)
    cols = lax.broadcasted_iota(jnp.int32, (K, K), 1)
    count = jnp.where(cols < rows, 2.0, jnp.where(cols == rows, 1.0, 0.0))
    low = 0.5 * beta * weight * count
    high = 0.5 * beta * (1.0 - weight) * count
    target = jnp.where(cols <= rows, target_ref[...], 0)
    for block in range(BLOCKS):
        n = B * (block + 1)
        tiles = n * B // K
        parts = [[None] * tiles for _ in range(3)]
        for jj in range(B):
            j = B * block + jj
            for which, array in enumerate((low, high, target)):
                row = array[j : j + 1]
                offset = jj * n
                first, shift = offset // K, offset % K
                if shift:
                    row = pltpu.roll(row, shift, 1)
                lane = cols[:1]
                pieces = [(first, row)]
                if shift + n > K:
                    zero = jnp.zeros_like(row)
                    pieces = [(first, jnp.where(lane >= shift, row, zero)), (first + 1, jnp.where(lane < shift, row, zero))]
                for tile, piece in pieces:
                    had = parts[which][tile]
                    parts[which][tile] = piece if had is None else had + piece
        top = K - B * block
        ks = lax.broadcasted_iota(jnp.int32, (top, K), 0) + B * block
        for tile in range(tiles):
            a, b, t = (parts[which][tile] for which in range(3))
            value = jnp.where(ks == t, a, jnp.where(ks == t + 1, b, 0.0))
            coef_refs[block][:, tile * K : (tile + 1) * K] = value.astype(BF16)


def prepare(kernel, split, target):
    shapes = [jax.ShapeDtypeStruct((K, K), BF16)]
    shapes += [jax.ShapeDtypeStruct((K - B * b, B * B * (b + 1)), BF16) for b in range(BLOCKS)]
    return pl.pallas_call(
        prepare_kernel,
        out_shape=shapes,
        in_specs=[VMEM] * 3,
        out_specs=[VMEM] * (BLOCKS + 1),
        compiler_params=params(16),
        name="prepare",
    )(kernel, split, target)


def reaction(planes, beta, coefs, pair_ref):
    x = jnp.concatenate(planes, axis=1) if len(planes) > 1 else planes[0]
    width = x.shape[1]
    low = x.astype(BF16)
    total = None
    for block in range(BLOCKS):
        n = B * (block + 1)
        for jj in range(B):
            j = B * block + jj
            factor = jnp.broadcast_to(x[j : j + 1], (B, width)).astype(BF16)
            for part in range(block + 1):
                at = jj * n + B * part
                pair_ref[at : at + B, :width] = low[B * part : B * (part + 1)] * factor
        gain = jnp.dot(coefs[block][...], pair_ref[: B * n, :width], preferred_element_type=F32)
        if block == 0:
            total = gain
        else:
            total = jnp.concatenate([total[: B * block], total[B * block :] + gain], axis=0)
    rate = jnp.dot(beta[...], low, preferred_element_type=F32)
    change = total - x * rate
    return [change[:, CELLS * p : CELLS * (p + 1)] for p in range(len(planes))]


def moved(before, here, after, speed_before, speed_here):
    out = jnp.maximum(speed_here, 0.0) * here + jnp.minimum(speed_here, 0.0) * after
    came = jnp.maximum(speed_before, 0.0) * before + jnp.minimum(speed_before, 0.0) * here
    return here - (out - came)


def unpack_kernel(core_ref, blocks_ref, speed_ref, state_ref, to_x_ref, to_s_ref):
    core = core_ref[0]
    for p in range(3):
        for d in range(16):
            state_ref[p, 8 * d : 8 * d + 8] = blocks_ref[d, p]
    for h in range(2):
        to_x_ref[h, :K] = state_ref[core + h]
        to_s_ref[h, :K] = state_ref[1 - core + h]
        to_x_ref[h, K:] = jnp.broadcast_to(speed_ref[pl.ds(core + h, 1)], (8, CELLS))
        to_s_ref[h, K:] = jnp.broadcast_to(speed_ref[pl.ds(1 - core + h, 1)], (8, CELLS))


def react_kernel(state_ref, beta_ref, *refs):
    coefs, change_ref, pair_ref = refs[:BLOCKS], refs[BLOCKS], refs[BLOCKS + 1]
    for p, change in enumerate(reaction([state_ref[p] for p in range(3)], beta_ref, coefs, pair_ref)):
        change_ref[p] = change


def react(state, beta, coefs):
    return pl.pallas_call(
        react_kernel,
        out_shape=jax.ShapeDtypeStruct((3, K, CELLS), F32),
        in_specs=[VMEM] * (2 + BLOCKS),
        out_specs=VMEM,
        scratch_shapes=[pltpu.VMEM((2048, 3 * CELLS), BF16)],
        compiler_params=params(24),
        cost_estimate=pl.CostEstimate(flops=2 * K * 9216 * 384, bytes_accessed=3000000, transcendentals=0),
        name="react",
    )(state, beta, *coefs)


def two_steps(core_ref, state_ref, change_ref, from_x_ref, from_s_ref, faces, beta_ref, coefs, pair_ref, all_ref):
    core = core_ref[0]
    for h in range(2):
        all_ref[5 * core + h] = from_x_ref[h, :K]
        all_ref[5 * (1 - core) + h] = from_s_ref[h, :K]
    first, last = reaction([all_ref[1], all_ref[5]], beta_ref, coefs, pair_ref)
    before, after = all_ref[0], all_ref[6]
    planes = [before, all_ref[1], *(state_ref[p] for p in range(3)), all_ref[5], after]
    changes = [None, first, *(change_ref[p] for p in range(3)), last]
    once = [moved(planes[p - 1], planes[p], planes[p + 1], faces[p - 1], faces[p]) + changes[p] for p in range(1, 6)]
    again = reaction(once[1:4], beta_ref, coefs, pair_ref)
    return [moved(once[q], once[q + 1], once[q + 2], faces[q + 1], faces[q + 2]) + again[q] for q in range(3)]


def first_kernel(core_ref, state_ref, change_ref, from_x_ref, from_s_ref, speed_ref, beta_ref, *refs):
    coefs = refs[:BLOCKS]
    out_ref, to_x_ref, to_s_ref, faces_ref, pair_ref, all_ref = refs[BLOCKS:]
    core = core_ref[0]
    for h in range(2):
        faces_ref[pl.ds(5 * core + h, 1)] = from_x_ref[h, K : K + 1]
        faces_ref[pl.ds(5 * (1 - core) + h, 1)] = from_s_ref[h, K : K + 1]
    faces_ref[2:5] = speed_ref[...]
    faces = [faces_ref[f : f + 1] for f in range(7)]
    states = two_steps(core_ref, state_ref, change_ref, from_x_ref, from_s_ref, faces, beta_ref, coefs, pair_ref, all_ref)
    for p in range(3):
        out_ref[p] = states[p]
    for h in range(2):
        to_x_ref[h] = out_ref[core + h]
        to_s_ref[h] = out_ref[1 - core + h]


def second_kernel(core_ref, state_ref, change_ref, from_x_ref, from_s_ref, faces_ref, beta_ref, *refs):
    coefs = refs[:BLOCKS]
    out_ref, pair_ref, all_ref = refs[BLOCKS:]
    faces = [faces_ref[f : f + 1] for f in range(7)]
    states = two_steps(core_ref, state_ref, change_ref, from_x_ref, from_s_ref, faces, beta_ref, coefs, pair_ref, all_ref)
    for p in range(3):
        for d in range(16):
            out_ref[d, p] = states[p][8 * d : 8 * d + 8]


def swap(array, odd):
    pairs = [(s, (s + 1) % 32) for s in range(32) if s % 2 == odd]
    return lax.ppermute(array, SPACE, pairs + [(b, a) for a, b in pairs])


def on_device(density, velocity, kernel, split, target):
    core = lax.axis_index("core").astype(jnp.int32).reshape(1)
    beta, *coefs = prepare(kernel, split, target)
    blocks = density.reshape(3, 8, 16, CELLS).transpose(2, 0, 1, 3)
    blocks = lax.all_to_all(blocks, SECT, split_axis=0, concat_axis=0, tiled=True)
    speed = lax.dynamic_slice_in_dim(velocity, lax.axis_index(SECT) * CELLS, CELLS, 1)
    plane, halo = jax.ShapeDtypeStruct((3, K, CELLS), F32), jax.ShapeDtypeStruct((2, K, CELLS), F32)
    wide = jax.ShapeDtypeStruct((2, K + 8, CELLS), F32)
    state, to_x, to_s = pl.pallas_call(
        unpack_kernel,
        out_shape=[plane, wide, wide],
        in_specs=[SMEM, VMEM, VMEM],
        out_specs=[VMEM] * 3,
        compiler_params=params(8),
        name="unpack",
    )(core, blocks, speed)
    scratch = [pltpu.VMEM((2048, 3 * CELLS), BF16), pltpu.VMEM((7, K, CELLS), F32)]

    from_x, from_s = swap(to_x, 1), swap(to_s, 0)
    change = react(state, beta, coefs)
    state, to_x, to_s, faces = pl.pallas_call(
        first_kernel,
        out_shape=[plane, halo, halo, jax.ShapeDtypeStruct((7, CELLS), F32)],
        in_specs=[SMEM] + [VMEM] * (6 + BLOCKS),
        out_specs=[VMEM] * 4,
        scratch_shapes=scratch,
        compiler_params=params(24),
        name="first_two",
    )(core, state, change, from_x, from_s, speed, beta, *coefs)

    from_x, from_s = swap(to_x, 1), swap(to_s, 0)
    change = react(state, beta, coefs)
    blocks = pl.pallas_call(
        second_kernel,
        out_shape=jax.ShapeDtypeStruct((16, 3, 8, CELLS), F32),
        in_specs=[SMEM] + [VMEM] * (6 + BLOCKS),
        out_specs=VMEM,
        scratch_shapes=scratch,
        compiler_params=params(24),
        name="last_two",
    )(core, state, change, from_x, from_s, faces, beta, *coefs)
    blocks = lax.all_to_all(blocks, SECT, split_axis=0, concat_axis=0, tiled=True)
    return blocks.transpose(1, 2, 0, 3).reshape(density.shape)


def solution(mesh):
    torus = Mesh(mesh.devices.reshape(16, 2, 2, 8), ("chip", "core", "zl", "y"))
    return jax.shard_map(
        on_device,
        mesh=torus,
        in_specs=(P(SPACE, SECT, None), P(SPACE, None), P(), P(), P()),
        out_specs=P(SPACE, SECT, None),
        check_vma=False,
    )
```

profile of v0, /device:TPU:8, one launch (start us, length us, event | category | flops | bytes accessed | tf_op | source)
XLA Modules:
  0.0 65.4 jit_solution(16379333547279738877)
XLA Ops:
  0.0 0.0 copy-start
  0.0 0.9 %copy-done = f32[3,8,2048]{2,1,0:T(8,128)S(1)} copy-done((f32[3,8,2048]{2,1,0:T(8,128)S(1)}, f32[3,8,2048]{2,1,0:T(8,128)}, u32[]{:S(2)}) %copy-start) | copy-done | bytes 196632
  0.9 0.7 %bitcast_bitcast_fusion = f32[16,3,8,128]{3,2,1,0:T(8,128)} fusion(f32[3,8,2048]{2,1,0:T(8,128)S(1)} %copy-done), kind=kLoop, calls=%fused_computation.1 | loop fusion | bytes 393216 | tf_op jit(solution)/shard_map/transpose | solution.py:186
  1.6 9.4 %all-to-all-start = ((f32[16,3,8,128]{3,2,1,0:T(8,128)}), f32[16,3,8,128]{3,2,1,0:T(8,128)S(1)}, u32[]{:S(2)}, u32[]{:S(2)}) async-start(f32[16,3,8,128]{3,2,1,0:T(8,128)} %bitcast_bitcast_fusion), calls=%async_computation | async-start | bytes 393216 | tf_op jit(solution)/shard_map/all_to_all | solution.py:187
  11.0 0.7 %constant_dynamic-slice_fusion.speed_ref = f32[3,128]{1,0:T(4,128)S(1)} fusion(f32[3,2048]{1,0:T(4,128)} %param.6, s32[]{:T(128)S(6)} %select_n.3), kind=kLoop, calls=%fused_computation.2 | loop fusion | bytes 3076 | tf_op jit(solution)/shard_map/dynamic_slice | solution.py:188
  11.7 8.5 %all-to-all-done.blocks_ref = f32[16,3,8,128]{3,2,1,0:T(8,128)S(1)} async-done(((f32[16,3,8,128]{3,2,1,0:T(8,128)}), f32[16,3,8,128]{3,2,1,0:T(8,128)S(1)}, u32[]{:S(2)}, u32[]{:S(2)}) %all-to-all-start) | async-done | bytes 196640 | tf_op jit(solution)/shard_map/all_to_all | solution.py:187
  20.2 9.7 %collective-permute-start = (f32[2,136,128]{2,1,0:T(8,128)S(1)}, f32[2,136,128]{2,1,0:T(8,128)S(1)}, u32[]{:S(2)}, u32[]{:S(2)}) collective-permute-start(f32[2,136,128]{2,1,0:T(8,128)S(1)} %get-tuple-element.31), channel_id=1, source_target_pairs={{16,32},{48,64},{80,96},{112,128},{144,160},{176,192},{208,224},{2... | collective-permute-start | bytes 417800 | tf_op jit(solution)/shard_map/ppermute | solution.py:180
  29.9 1.9 %collective-permute-start.1 = (f32[2,136,128]{2,1,0:T(8,128)S(1)}, f32[2,136,128]{2,1,0:T(8,128)S(1)}, u32[]{:S(2)}, u32[]{:S(2)}) collective-permute-start(f32[2,136,128]{2,1,0:T(8,128)S(1)} %get-tuple-element.32), channel_id=1, source_target_pairs={{0,16},{32,48},{64,80},{96,112},{128,144},{160,176},{192,208},{224... | collective-permute-start | bytes 417800 | tf_op jit(solution)/shard_map/ppermute | solution.py:180
  31.9 0.0 copy-done.1
  31.9 0.0 copy-done.2
  31.9 0.0 copy-done.3
  31.9 0.7 %prepare.1 = (bf16[128,128]{1,0:T(8,128)(2,1)S(1)}, bf16[128,256]{1,0:T(8,128)(2,1)S(1)}, bf16[112,512]{1,0:T(8,128)(2,1)S(1)}, bf16[96,768]{1,0:T(8,128)(2,1)S(...) custom-call(f32[128,128]{1,0:T(8,128)S(1)} %copy-done.1, ...), custom_call_target="tpu_custom_call" | custom-call | tf_op jit(solution)/shard_map/prepare/pallas_call | solution.py:67
  32.6 1.5 %react.2.change_ref = f32[3,128,128]{2,1,0:T(8,128)S(1)} custom-call(f32[3,128,128]{2,1,0:T(8,128)S(1)} %get-tuple-element.21.state_ref, bf16[128,128]{1,0:T(8,128)(2,1)S(1)} %get-tuple-element.22.beta_ref, bf16[128,256]{1,0:T(8,128)(2,1)S(1)} %get-tuple-element.23.refs_0_, bf16[112,512]{1,0:T(8,128)(2,1)S(1)} %get-tuple-element.24.refs_1_, ...), custom_call_target="tpu_custom_call" | custom-call | flops 905969664 | bytes 3000000 | tf_op jit(solution)/shard_map/react/pallas_call | solution.py:125
  34.2 0.0 collective-permute-done.from_x_ref
  34.2 0.0 collective-permute-done.1.from_s_ref
  34.2 2.3 %first_two.1 = (f32[3,128,128]{2,1,0:T(8,128)S(1)}, f32[2,128,128]{2,1,0:T(8,128)S(1)}, f32[2,128,128]{2,1,0:T(8,128)S(1)}, f32[7,128]{1,0:T(8,128)S(1)}) custom-call(s32[1]{0:T(128)} %bitcast.core_ref, f32[3,128,128]{2,1,0:T(8,128)S(1)} %get-tuple-element.21.state_ref, f32[3,128,128]{2,1,0:T(8,128)S(1)} %react.2.change_ref, ...), custom_call_target="tpu_custom_call" | custom-call | tf_op jit(solution)/shard_map/first_two/pallas_call | solution.py:203
  36.5 7.8 %collective-permute-start.2 = (f32[2,128,128]{2,1,0:T(8,128)S(1)}, f32[2,128,128]{2,1,0:T(8,128)S(1)}, u32[]{:S(2)}, u32[]{:S(2)}) collective-permute-start(f32[2,128,128]{2,1,0:T(8,128)S(1)} %get-tuple-element.34), channel_id=1, source_target_pairs={{16,32},{48,64},{80,96},{112,128},{144,160},{176,192},{208,224},{2... | collective-permute-start | bytes 393224 | tf_op jit(solution)/shard_map/ppermute | solution.py:180
  44.3 1.9 %collective-permute-start.3 = (f32[2,128,128]{2,1,0:T(8,128)S(1)}, f32[2,128,128]{2,1,0:T(8,128)S(1)}, u32[]{:S(2)}, u32[]{:S(2)}) collective-permute-start(f32[2,128,128]{2,1,0:T(8,128)S(1)} %get-tuple-element.35), channel_id=1, source_target_pairs={{0,16},{32,48},{64,80},{96,112},{128,144},{160,176},{192,208},{224... | collective-permute-start | bytes 393224 | tf_op jit(solution)/shard_map/ppermute | solution.py:180
  46.3 1.5 %react.3.change_ref = f32[3,128,128]{2,1,0:T(8,128)S(1)} custom-call(f32[3,128,128]{2,1,0:T(8,128)S(1)} %get-tuple-element.33.state_ref, bf16[128,128]{1,0:T(8,128)(2,1)S(1)} %get-tuple-element.22.beta_ref, bf16[128,256]{1,0:T(8,128)(2,1)S(1)} %get-tuple-element.23.refs_0_, bf16[112,512]{1,0:T(8,128)(2,1)S(1)} %get-tuple-element.24.refs_1_, ...), custom_call_target="tpu_custom_call" | custom-call | flops 905969664 | bytes 3000000 | tf_op jit(solution)/shard_map/react/pallas_call | solution.py:125
  47.8 0.3 collective-permute-done.2.from_x_ref
  48.1 0.0 collective-permute-done.3.from_s_ref
  48.1 2.2 %last_two.1 = f32[16,3,8,128]{3,2,1,0:T(8,128)S(1)} custom-call(s32[1]{0:T(128)} %bitcast.core_ref, f32[3,128,128]{2,1,0:T(8,128)S(1)} %get-tuple-element.33.state_ref, f32[3,128,128]{2,1,0:T(8,128)S(1)} %react.3.change_ref, f32[2,128,128]{2,1,0:T(8,128)S(1)} %collective-permute-done.2.from_x_ref, f32[2,128,128]{2,1,0:T(8,128)S(1)} %collective-permute-done.3.from_s_ref, ...), custom_call_target="tpu_custom_call" | custom-call | tf_op jit(solution)/shard_map/last_two/pallas_call | solution.py:215
  50.3 14.4 %all_to_all.10 = f32[16,3,8,128]{3,2,1,0:T(8,128)S(1)} all-to-all(f32[16,3,8,128]{3,2,1,0:T(8,128)S(1)} %last_two.1), channel_id=1, replica_groups=mesh['chip'=16,'core'=2,'zl'=2,'y'=8] {'zl','y'}, dimensions={0} | all-to-all | bytes 393216 | tf_op jit(solution)/shard_map/all_to_all | solution.py:224
  64.7 0.7 %copy_bitcast_fusion = f32[3,8,2048]{2,1,0:T(8,128)} fusion(f32[16,3,8,128]{3,2,1,0:T(8,128)S(1)} %all_to_all.10), kind=kLoop, calls=%fused_computation | loop fusion | bytes 393216 | tf_op jit(solution)/shard_map/reshape | solution.py:225
  (4 shorter events, 0.0 us)
Async XLA Ops:
  0.0 0.9 %copy-start = (f32[3,8,2048]{2,1,0:T(8,128)S(1)}, f32[3,8,2048]{2,1,0:T(8,128)}, u32[]{:S(2)}) copy-start(f32[3,8,2048]{2,1,0:T(8,128)} %param.5) | copy-start | bytes 589828
  1.6 18.6 %all-to-all-start = ((f32[16,3,8,128]{3,2,1,0:T(8,128)}), f32[16,3,8,128]{3,2,1,0:T(8,128)S(1)}, u32[]{:S(2)}, u32[]{:S(2)}) async-start(f32[16,3,8,128]{3,2,1,0:T(8,128)} %bitcast_bitcast_fusion), calls=%async_computation | async-start | bytes 393216 | tf_op jit(solution)/shard_map/all_to_all | solution.py:187
  20.2 11.7 %copy-start.1 = (f32[128,128]{1,0:T(8,128)S(1)}, f32[128,128]{1,0:T(8,128)}, u32[]{:S(2)}) copy-start(f32[128,128]{1,0:T(8,128)} %kernel_ref.1) | copy-start | bytes 196612
  20.2 11.7 %copy-start.2 = (f32[128,128]{1,0:T(8,128)S(1)}, f32[128,128]{1,0:T(8,128)}, u32[]{:S(2)}) copy-start(f32[128,128]{1,0:T(8,128)} %split_ref.1) | copy-start | bytes 196612
  20.2 11.7 %copy-start.3 = (s32[128,128]{1,0:T(8,128)S(1)}, s32[128,128]{1,0:T(8,128)}, u32[]{:S(2)}) copy-start(s32[128,128]{1,0:T(8,128)} %target_ref.1) | copy-start | bytes 196612
  20.2 13.9 %collective-permute-start = (f32[2,136,128]{2,1,0:T(8,128)S(1)}, f32[2,136,128]{2,1,0:T(8,128)S(1)}, u32[]{:S(2)}, u32[]{:S(2)}) collective-permute-start(f32[2,136,128]{2,1,0:T(8,128)S(1)} %get-tuple-element.31), channel_id=1, source_target_pairs={{16,32},{48,64},{80,96},{112,128},{144,160},{176,192},{208,224},{2... | collective-permute-start | bytes 417800 | tf_op jit(solution)/shard_map/ppermute | solution.py:180
  29.9 4.2 %collective-permute-start.1 = (f32[2,136,128]{2,1,0:T(8,128)S(1)}, f32[2,136,128]{2,1,0:T(8,128)S(1)}, u32[]{:S(2)}, u32[]{:S(2)}) collective-permute-start(f32[2,136,128]{2,1,0:T(8,128)S(1)} %get-tuple-element.32), channel_id=1, source_target_pairs={{0,16},{32,48},{64,80},{96,112},{128,144},{160,176},{192,208},{224... | collective-permute-start | bytes 417800 | tf_op jit(solution)/shard_map/ppermute | solution.py:180
  36.5 11.6 %collective-permute-start.2 = (f32[2,128,128]{2,1,0:T(8,128)S(1)}, f32[2,128,128]{2,1,0:T(8,128)S(1)}, u32[]{:S(2)}, u32[]{:S(2)}) collective-permute-start(f32[2,128,128]{2,1,0:T(8,128)S(1)} %get-tuple-element.34), channel_id=1, source_target_pairs={{16,32},{48,64},{80,96},{112,128},{144,160},{176,192},{208,224},{2... | collective-permute-start | bytes 393224 | tf_op jit(solution)/shard_map/ppermute | solution.py:180
  44.3 3.8 %collective-permute-start.3 = (f32[2,128,128]{2,1,0:T(8,128)S(1)}, f32[2,128,128]{2,1,0:T(8,128)S(1)}, u32[]{:S(2)}, u32[]{:S(2)}) collective-permute-start(f32[2,128,128]{2,1,0:T(8,128)S(1)} %get-tuple-element.35), channel_id=1, source_target_pairs={{0,16},{32,48},{64,80},{96,112},{128,144},{160,176},{192,208},{224... | collective-permute-start | bytes 393224 | tf_op jit(solution)/shard_map/ppermute | solution.py:180
where the time goes:
time: 65.8 us; the launch traced here: 65.4 us
  starting transfers between devices  30.8 us (47%)
  blocking collectives  14.4 us (22%)
  waiting for transfers between devices  8.8 us (13%)
  Pallas kernels  8.34 us (13%)
  local copies, waits for them, and re-layouts  3 us (5%)
    ppermute x4, starting transfers between devices, swap(): return lax.ppermute(array, SPACE, pairs + [(b, a) for a, b in pairs])  21.4 us
    all_to_all x1, blocking collectives, on_device(): lax.all_to_all(blocks, SECT, split_axis=0, concat_axis=0, tiled=True)  14.4 us
    all_to_all x1, starting transfers between devices, on_device(): lax.all_to_all(blocks, SECT, split_axis=0, concat_axis=0, tiled=True)  9.37 us
    all_to_all x1, waiting for transfers between devices, on_device(): lax.all_to_all(blocks, SECT, split_axis=0, concat_axis=0, tiled=True)  8.52 us
    pallas_call x2, Pallas kernels, react(): pl.pallas_call(react_kernel, out_shape=jax.ShapeDtypeStruct((3, K, CELLS)...  3.08 us
    pallas_call x1, Pallas kernels, on_device(): pl.pallas_call(first_kernel, out_shape=[plane, halo, halo, jax.ShapeDtype...  2.29 us
    pallas_call x1, Pallas kernels, on_device(): pl.pallas_call(second_kernel, out_shape=jax.ShapeDtypeStruct((16, 3, 8, C...  2.24 us
  transfers between devices with their start and end apart: 5, of which 2 were waited for; matrix products, arithmetic and copies ran while one was open for 1% of the time, Pallas kernels for 6%

commit v1 on v0

v1 whole, which is shorter than its diff:
```python
import jax
import jax.numpy as jnp
from jax import lax
from jax.experimental import pallas as pl
from jax.experimental.pallas import tpu as pltpu
from jax.sharding import Mesh
from jax.sharding import PartitionSpec as P

K = 128
CELLS = 128
BLOCKS = 8
B = 16
SECT = ("zl", "y")
SPACE = ("chip", "core")
STEPS = 4
VMEM = pl.BlockSpec(memory_space=pltpu.VMEM)
SMEM = pl.BlockSpec(memory_space=pltpu.SMEM)
F16 = jnp.float16
F32 = jnp.float32
BF16 = jnp.bfloat16


def params(mib):
    return pltpu.CompilerParams(vmem_limit_bytes=mib * 1024 * 1024)


def prepare_kernel(kernel_ref, split_ref, target_ref, beta_ref, *coef_refs):
    kernel, split = kernel_ref[...], split_ref[...]
    beta = 0.5 * (kernel + kernel.T)
    weight = 0.5 * (split + split.T)
    beta_ref[...] = beta.astype(BF16)
    rows = lax.broadcasted_iota(jnp.int32, (K, K), 0)
    cols = lax.broadcasted_iota(jnp.int32, (K, K), 1)
    count = jnp.where(cols < rows, 2.0, jnp.where(cols == rows, 1.0, 0.0))
    low = 0.5 * beta * weight * count
    high = 0.5 * beta * (1.0 - weight) * count
    target = jnp.where(cols <= rows, target_ref[...], 0)
    for block in range(BLOCKS):
        n = B * (block + 1)
        tiles = n * B // K
        parts = [[None] * tiles for _ in range(3)]
        for jj in range(B):
            j = B * block + jj
            for which, array in enumerate((low, high, target)):
                row = array[j : j + 1]
                offset = jj * n
                first, shift = offset // K, offset % K
                if shift:
                    row = pltpu.roll(row, shift, 1)
                lane = cols[:1]
                pieces = [(first, row)]
                if shift + n > K:
                    zero = jnp.zeros_like(row)
                    pieces = [(first, jnp.where(lane >= shift, row, zero)), (first + 1, jnp.where(lane < shift, row, zero))]
                for tile, piece in pieces:
                    had = parts[which][tile]
                    parts[which][tile] = piece if had is None else had + piece
        top = K - B * block
        ks = lax.broadcasted_iota(jnp.int32, (top, K), 0) + B * block
        for tile in range(tiles):
            a, b, t = (parts[which][tile] for which in range(3))
            value = jnp.where(ks == t, a, jnp.where(ks == t + 1, b, 0.0))
            coef_refs[block][:, tile * K : (tile + 1) * K] = value.astype(BF16)


def prepare(kernel, split, target):
    shapes = [jax.ShapeDtypeStruct((K, K), BF16)]
    shapes += [jax.ShapeDtypeStruct((K - B * b, B * B * (b + 1)), BF16) for b in range(BLOCKS)]
    return pl.pallas_call(
        prepare_kernel,
        out_shape=shapes,
        in_specs=[VMEM] * 3,
        out_specs=[VMEM] * (BLOCKS + 1),
        compiler_params=params(16),
        name="prepare",
    )(kernel, split, target)


def reaction(planes, beta, coefs, pair_ref):
    x = jnp.concatenate(planes, axis=1) if len(planes) > 1 else planes[0]
    width = x.shape[1]
    low = x.astype(BF16)
    total = None
    for block in range(BLOCKS):
        n = B * (block + 1)
        for jj in range(B):
            j = B * block + jj
            factor = jnp.broadcast_to(x[j : j + 1], (B, width)).astype(BF16)
            for part in range(block + 1):
                at = jj * n + B * part
                pair_ref[at : at + B, :width] = low[B * part : B * (part + 1)] * factor
        gain = jnp.dot(coefs[block][...], pair_ref[: B * n, :width], preferred_element_type=F32)
        if block == 0:
            total = gain
        else:
            total = jnp.concatenate([total[: B * block], total[B * block :] + gain], axis=0)
    rate = jnp.dot(beta[...], low, preferred_element_type=F32)
    change = total - x * rate
    return [change[:, CELLS * p : CELLS * (p + 1)] for p in range(len(planes))]


def moved(before, here, after, speed_before, speed_here):
    out = jnp.maximum(speed_here, 0.0) * here + jnp.minimum(speed_here, 0.0) * after
    came = jnp.maximum(speed_before, 0.0) * before + jnp.minimum(speed_before, 0.0) * here
    return here - (out - came)


def steps_kernel(core_ref, chip_ref, far_ref, near_ref, beta_ref, *refs):
    coefs, out_ref, pair_ref, window_ref = refs[:BLOCKS], refs[BLOCKS], refs[BLOCKS + 1], refs[BLOCKS + 2]
    core = core_ref[0]
    for p in range(4):
        window_ref[7 * core + p] = far_ref[p]
    for p in range(6):
        window_ref[4 - 3 * core + p] = chip_ref[p]
    window_ref[10 * (1 - core)] = near_ref[...]
    planes = [window_ref[w, :K] for w in range(11)]
    faces = [window_ref[w, K : K + 1] + window_ref[w, K + 1 : K + 2] * (1.0 / 2048.0) for w in range(11)]
    for step in range(STEPS):
        inner = range(1, len(planes) - 1)
        changes = reaction([planes[w] for w in inner], beta_ref, coefs, pair_ref)
        planes = [
            moved(planes[w - 1], planes[w], planes[w + 1], faces[w - 1 + step], faces[w + step]) + changes[w - 1]
            for w in inner
        ]
    for p in range(3):
        for d in range(16):
            out_ref[d, p] = planes[p][8 * d : 8 * d + 8] * (1.0 / 512.0)


def on_device(density, velocity, kernel, split, target):
    core = lax.axis_index("core").astype(jnp.int32)
    beta, *coefs = prepare(kernel, split, target)
    blocks = density.reshape(3, 8, 16, CELLS).transpose(2, 0, 1, 3).astype(F16)
    blocks = lax.all_to_all(blocks, SECT, split_axis=0, concat_axis=0, tiled=True)
    speed = lax.dynamic_slice_in_dim(velocity, lax.axis_index(SECT) * CELLS, CELLS, 1)
    high = speed.astype(F16)
    rest = ((speed - high.astype(F32)) * 2048.0).astype(F16)
    own = blocks.transpose(1, 0, 2, 3).reshape(3, K, CELLS)
    own = jnp.concatenate([own, high[:, None], rest[:, None], jnp.zeros((3, 14, CELLS), F16)], axis=1)
    chip = lax.all_gather(own, "core", axis=0, tiled=True)
    edge = lax.dynamic_slice_in_dim(chip, 2 * core, 4, 0)
    neighbours = [[s, (s + 1) % 32] for s in range(1, 32, 2)]
    far = lax.all_gather(edge, SPACE, axis=0, axis_index_groups=neighbours)
    far = lax.dynamic_index_in_dim(far, core, 0, keepdims=False)
    near = lax.all_gather(lax.dynamic_index_in_dim(far, 3 * (1 - core), 0, keepdims=False), "core", axis=0)
    near = lax.dynamic_index_in_dim(near, 1 - core, 0, keepdims=False)
    blocks = pl.pallas_call(
        steps_kernel,
        out_shape=jax.ShapeDtypeStruct((16, 3, 8, CELLS), F32),
        in_specs=[SMEM] + [VMEM] * (4 + BLOCKS),
        out_specs=VMEM,
        scratch_shapes=[pltpu.VMEM((2048, 9 * CELLS), BF16), pltpu.VMEM((11, K + 16, CELLS), F32)],
        compiler_params=params(32),
        name="steps",
    )(core.reshape(1), chip.astype(F32), far.astype(F32), near.astype(F32), beta, *coefs)
    blocks = lax.all_to_all(blocks.astype(F16), SECT, split_axis=0, concat_axis=0, tiled=True)
    return blocks.transpose(1, 2, 0, 3).reshape(density.shape).astype(F32) * 512.0


def solution(mesh):
    torus = Mesh(mesh.devices.reshape(16, 2, 2, 8), ("chip", "core", "zl", "y"))
    return jax.shard_map(
        on_device,
        mesh=torus,
        in_specs=(P(SPACE, SECT, None), P(SPACE, None), P(), P(), P()),
        out_specs=P(SPACE, SECT, None),
        check_vma=False,
    )
```

time: 65.8 us -> 61.5 us (0.935)
  the two profiles are of different devices: /device:TPU:8 before, /device:TPU:1 now
where the time goes in v1:
time: 61.5 us; the launch traced here: 61.1 us
  blocking collectives  30.5 us (50%)
  Pallas kernels  11.5 us (19%)
  starting transfers between devices  9.69 us (16%)
  waiting for transfers between devices  5.96 us (10%)
  other arithmetic  2.5 us (4%)
  local copies, waits for them, and re-layouts  0.92 us (1%)
    pallas_call x1, Pallas kernels, on_device(): pl.pallas_call(steps_kernel, out_shape=jax.ShapeDtypeStruct((16, 3, 8, CE...  10.8 us
    all_to_all x1, blocking collectives, on_device(): lax.all_to_all(blocks.astype(F16), SECT, split_axis=0, concat_axis=0, til...  9.98 us
    all_to_all x1, starting transfers between devices, on_device(): lax.all_to_all(blocks, SECT, split_axis=0, concat_axis=0, tiled=True)  9.69 us
    all_gather x1, blocking collectives, on_device(): far = lax.all_gather(edge, SPACE, axis=0, axis_index_groups=neighbours)  9.21 us
    all_gather x1, blocking collectives, on_device(): lax.all_gather(lax.dynamic_index_in_dim(far, 3 * (1 - core), 0, keepdims=...  7.69 us
    all_to_all x1, waiting for transfers between devices, on_device(): lax.all_to_all(blocks, SECT, split_axis=0, concat_axis=0, tiled=True)  5.96 us
    all_gather x1, blocking collectives, on_device(): chip = lax.all_gather(own, 'core', axis=0, tiled=True)  3.62 us
  transfers between devices with their start and end apart: 1, of which 1 were waited for; matrix products, arithmetic and copies ran while one was open for 1% of the time, Pallas kernels for 1%

profile of v1, /device:TPU:1, one launch (start us, length us, event | category | flops | bytes accessed | tf_op | source)
XLA Modules:
  0.0 61.1 jit_solution(5767422278964781396)
XLA Ops:
  0.0 0.9 %convert_bitcast_fusion = f16[3,8,16,128]{3,1,2,0:T(8,128)(2,1)S(1)} fusion(f32[3,8,2048]{2,1,0:T(8,128)} %param.5), kind=kLoop, calls=%fused_computation.6 | loop fusion | flops 49152 | bytes 294912
  1.0 0.7 %copy.15 = f16[16,3,8,128]{3,2,1,0:T(8,128)(2,1)} copy(f16[16,3,8,128]{3,0,2,1:T(8,128)(2,1)S(1)} %bitcast.36) | data formatting | bytes 196608 | tf_op jit(solution)/shard_map/convert_element_type | solution.py:133
  1.7 0.0 copy-start.1
  1.7 0.0 copy-start.2
  1.7 9.7 %all-to-all-start = ((f16[16,3,8,128]{3,2,1,0:T(8,128)(2,1)}), f16[16,3,8,128]{3,2,1,0:T(8,128)(2,1)S(1)}, u32[]{:S(2)}, u32[]{:S(2)}) async-start(f16[16,3,8,128]{3,2,1,0:T(8,128)(2,1)} %copy.15), calls=%async_computation | async-start | bytes 196608 | tf_op jit(solution)/shard_map/all_to_all | solution.py:134
  11.4 0.0 copy-start
  11.4 0.7 %fusion.1 = (f16[3,1,128]{2,0,1:T(4,128)(2,1)S(1)}, f16[3,1,128]{2,0,1:T(4,128)(2,1)S(1)}) fusion(f32[3,2048]{1,0:T(4,128)} %param.6, s32[]{:T(128)S(6)} %select_n.22), kind=kLoop, calls=%fused_computation.13 | loop fusion | flops 1920 | bytes 3076 | tf_op jit(solution)/shard_map/broadcast_in_dim | solution.py:139
  12.1 0.1 pad.3.clone
  12.2 0.0 copy-done.1
  12.2 0.0 copy-done.2
  12.2 0.0 copy-done
  12.2 0.7 %prepare.1 = (bf16[128,128]{1,0:T(8,128)(2,1)S(1)}, bf16[128,256]{1,0:T(8,128)(2,1)S(1)}, bf16[112,512]{1,0:T(8,128)(2,1)S(1)}, bf16[96,768]{1,0:T(8,128)(2,1)S(...) custom-call(f32[128,128]{1,0:T(8,128)S(1)} %copy-done, ...), custom_call_target="tpu_custom_call" | custom-call | tf_op jit(solution)/shard_map/prepare/pallas_call | solution.py:69
  12.9 6.0 %all-to-all-done = f16[16,3,8,128]{3,2,1,0:T(8,128)(2,1)S(1)} async-done(((f16[16,3,8,128]{3,2,1,0:T(8,128)(2,1)}), f16[16,3,8,128]{3,2,1,0:T(8,128)(2,1)S(1)}, u32[]{:S(2)}, u32[]{:S(2)}) %all-to-all-start) | async-done | bytes 98336 | tf_op jit(solution)/shard_map/all_to_all | solution.py:134
  18.9 0.1 maximum_maximum_fusion
  19.0 3.6 %all_gather.13 = f16[6,144,128]{2,1,0:T(8,128)(2,1)S(1)} all-gather(f16[3,144,128]{2,1,0:T(8,128)(2,1)S(1)} %maximum_maximum_fusion), channel_id=1, replica_groups=mesh['chip'=16,'core'=2,'zl'=2,'y'=8] {'core'}, dimensions={0}, use_global_device_ids=true | all-gather | bytes 331776 | tf_op jit(solution)/shard_map/all_gather | solution.py:140
  22.7 9.2 %all-gather = f16[8,144,128]{2,1,0:T(8,128)(2,1)S(1)} all-gather(f16[4,144,128]{2,1,0:T(8,128)(2,1)S(1)} %constant_dynamic-slice_fusion.1), channel_id=2, replica_groups={{16,32},{48,64},{80,96},{112,128},{144,160},{176,192},{208,224},{240,25..., dimensions={0}, use_global_device_ids=true | all-gather | bytes 442368 | tf_op jit(solution)/shard_map/all_gather | solution.py:143
  32.0 7.7 %all-gather.1 = f16[2,1,144,128]{3,2,1,0:T(8,128)(2,1)S(1)} all-gather(f16[1,1,144,128]{3,2,1,0:T(8,128)(2,1)S(1)} %constant_dynamic-slice_fusion), channel_id=3, replica_groups=mesh['chip'=16,'core'=2,'zl'=2,'y'=8] {'core'}, dimensions={0}, use_global_device_ids=true | all-gather | bytes 110592 | tf_op jit(solution)/shard_map/all_gather | solution.py:145
  39.7 10.8 %steps.1 = f32[16,3,8,128]{3,2,1,0:T(8,128)S(1)} custom-call(s32[1]{0:T(128)} %bitcast.core_ref, f32[6,144,128]{2,1,0:T(8,128)S(1)} %convert_element_type.45.chip_ref, f32[4,144,128]{2,1,0:T(8,128)S(1)} %bitcast_convert_fusion.far_ref, f32[144,128]{1,0:T(8,128)S(1)} %bitcast_convert_fusion.1.near_ref, bf16[128,128]{1,0:T(8,128)(2,1)S(1)} %get-tuple-element.14.beta_ref, ...), custom_call_target="tpu_custom_call" | custom-call | tf_op jit(solution)/shard_map/steps/pallas_call | solution.py:147
  50.5 10.0 %all_to_all.10 = f16[16,3,8,128]{3,2,1,0:T(8,128)(2,1)S(1)} all-to-all(f16[16,3,8,128]{3,2,1,0:T(8,128)(2,1)S(1)} %convert_element_type.50), channel_id=1, replica_groups=mesh['chip'=16,'core'=2,'zl'=2,'y'=8] {'zl','y'}, dimensions={0} | all-to-all | bytes 196608 | tf_op jit(solution)/shard_map/all_to_all | solution.py:156
  60.4 0.7 %copy_bitcast_fusion = f32[3,8,2048]{2,1,0:T(8,128)} fusion(f16[16,3,8,128]{3,2,1,0:T(8,128)(2,1)S(1)} %all_to_all.10), kind=kLoop, calls=%fused_computation | loop fusion | flops 98304 | bytes 294912 | tf_op jit(solution)/shard_map/mul | solution.py:157
  (11 shorter events, 0.2 us)
Async XLA Ops:
  1.7 10.5 %copy-start.1 = (f32[128,128]{1,0:T(8,128)S(1)}, f32[128,128]{1,0:T(8,128)}, u32[]{:S(2)}) copy-start(f32[128,128]{1,0:T(8,128)} %split_ref.1) | copy-start | bytes 196612
  1.7 10.5 %copy-start.2 = (s32[128,128]{1,0:T(8,128)S(1)}, s32[128,128]{1,0:T(8,128)}, u32[]{:S(2)}) copy-start(s32[128,128]{1,0:T(8,128)} %target_ref.1) | copy-start | bytes 196612
  1.7 17.2 %all-to-all-start = ((f16[16,3,8,128]{3,2,1,0:T(8,128)(2,1)}), f16[16,3,8,128]{3,2,1,0:T(8,128)(2,1)S(1)}, u32[]{:S(2)}, u32[]{:S(2)}) async-start(f16[16,3,8,128]{3,2,1,0:T(8,128)(2,1)} %copy.15), calls=%async_computation | async-start | bytes 196608 | tf_op jit(solution)/shard_map/all_to_all | solution.py:134
  11.4 0.8 %copy-start = (f32[128,128]{1,0:T(8,128)S(1)}, f32[128,128]{1,0:T(8,128)}, u32[]{:S(2)}) copy-start(f32[128,128]{1,0:T(8,128)} %kernel_ref.1) | copy-start | bytes 196612

commit v2 on v1

--- a/solution.py
+++ b/solution.py
@@ -105,26 +105,74 @@
     return here - (out - came)
 
 
-def steps_kernel(core_ref, chip_ref, far_ref, near_ref, beta_ref, *refs):
-    coefs, out_ref, pair_ref, window_ref = refs[:BLOCKS], refs[BLOCKS], refs[BLOCKS + 1], refs[BLOCKS + 2]
+def inner_kernel(core_ref, chip_ref, beta_ref, *refs):
+    coefs, outs, (pair_ref, speed_ref) = refs[:BLOCKS], refs[BLOCKS:-2], refs[-2:]
+    react1_ref, state1_ref, react2_ref, state2_ref, react3_ref = outs
     core = core_ref[0]
+    sign = (1 - 2 * core).astype(F32)
+    planes = [chip_ref[5 * core + (1 - 2 * core) * p, :K] for p in range(6)]
+    for p in range(6):
+        speed_ref[p : p + 1] = chip_ref[p, K : K + 1] + chip_ref[p, K + 1 : K + 2] * (1.0 / 2048.0)
+    faces = [sign * speed_ref[pl.ds(4 * core + (1 - 2 * core) * f, 1)] for f in range(5)]
+    changes = reaction(planes, beta_ref, coefs, pair_ref)
+    react1_ref[0], react1_ref[1] = changes[0], changes[5]
+    planes = [moved(*planes[p - 1 : p + 2], faces[p - 1], faces[p]) + changes[p] for p in range(1, 5)]
     for p in range(4):
-        window_ref[7 * core + p] = far_ref[p]
+        state1_ref[p] = planes[p]
+    changes = reaction(planes, beta_ref, coefs, pair_ref)
+    react2_ref[0], react2_ref[1] = changes[0], changes[3]
+    planes = [moved(*planes[p - 1 : p + 2], faces[p], faces[p + 1]) + changes[p] for p in range(1, 3)]
+    changes = reaction(planes, beta_ref, coefs, pair_ref)
+    for p in range(2):
+        state2_ref[p] = planes[p]
+        react3_ref[p] = changes[p]
+
+
+def outer_kernel(core_ref, chip_ref, far_ref, near_ref, react1_ref, state1_ref, react2_ref, state2_ref, react3_ref, beta_ref, *refs):
+    coefs, out_ref, pair_ref, speed_ref = refs[:BLOCKS], refs[BLOCKS], refs[BLOCKS + 1], refs[BLOCKS + 2]
+    core = core_ref[0]
+    step = 1 - 2 * core
+    sign = step.astype(F32)
+
+    def speed(ref, p):
+        return ref[p, K : K + 1] + ref[p, K + 1 : K + 2] * (1.0 / 2048.0)
+
+    for p in range(4):
+        speed_ref[p : p + 1] = speed(far_ref, 3 * core + step * p)
     for p in range(6):
-        window_ref[4 - 3 * core + p] = chip_ref[p]
-    window_ref[10 * (1 - core)] = near_ref[...]
-    planes = [window_ref[w, :K] for w in range(11)]
-    faces = [window_ref[w, K : K + 1] + window_ref[w, K + 1 : K + 2] * (1.0 / 2048.0) for w in range(11)]
-    for step in range(STEPS):
-        inner = range(1, len(planes) - 1)
-        changes = reaction([planes[w] for w in inner], beta_ref, coefs, pair_ref)
-        planes = [
-            moved(planes[w - 1], planes[w], planes[w + 1], faces[w - 1 + step], faces[w + step]) + changes[w - 1]
-            for w in inner
-        ]
+        speed_ref[4 + p : 5 + p] = speed(chip_ref, 5 * core + step * p)
+    speed_ref[10:11] = near_ref[K : K + 1] + near_ref[K + 1 : K + 2] * (1.0 / 2048.0)
+    faces = [sign * speed_ref[pl.ds(core + f, 1)] for f in range(10)]
+
+    def advanced(state, change, w):
+        return moved(state[w - 1], state[w], state[w + 1], faces[w - 1], faces[w]) + change[w]
+
+    state = {w: far_ref[3 * core + step * w, :K] for w in range(4)}
+    state.update({4 + p: chip_ref[5 * core + step * p, :K] for p in range(6)})
+    state[10] = near_ref[:K]
+    known_changes = [{4: react1_ref[0], 9: react1_ref[1]}, {5: react2_ref[0], 8: react2_ref[1]}, {6: react3_ref[0], 7: react3_ref[1]}, {}]
+    known_states = [{5 + p: state1_ref[p] for p in range(4)}, {6 + p: state2_ref[p] for p in range(2)}, {}, {}]
+    for t in range(STEPS):
+        reacting = range(t + 1, t + 4)
+        change = dict(zip(reacting, reaction([state[w] for w in reacting], beta_ref, coefs, pair_ref)))
+        change.update(known_changes[t])
+        after = dict(known_states[t])
+        for w in range(t + 1, 10 - t):
+            if w not in after:
+                after[w] = advanced(state, change, w)
+        state = after
     for p in range(3):
+        value = state[4 + p] * (1.0 / 512.0)
         for d in range(16):
-            out_ref[d, p] = planes[p][8 * d : 8 * d + 8] * (1.0 / 512.0)
+            out_ref[d, 2 * core + step * p] = value[8 * d : 8 * d + 8]
+
+
+def scratch(planes, rows):
+    return [pltpu.VMEM((2048, planes * CELLS), BF16)] + [pltpu.VMEM((r, CELLS), F32) for r in rows]
+
+
+def cost(planes):
+    return pl.CostEstimate(flops=2 * K * 9216 * CELLS * planes, bytes_accessed=3000000, transcendentals=0)
 
 
 def on_device(density, velocity, kernel, split, target):
@@ -137,22 +185,35 @@
     rest = ((speed - high.astype(F32)) * 2048.0).astype(F16)
     own = blocks.transpose(1, 0, 2, 3).reshape(3, K, CELLS)
     own = jnp.concatenate([own, high[:, None], rest[:, None], jnp.zeros((3, 14, CELLS), F16)], axis=1)
+    side = [((s + 2) % 32, s) if s % 2 == 0 else (s, (s + 2) % 32) for s in range(32)]
+    near = lax.ppermute(lax.dynamic_index_in_dim(own, 2 * core, 0, keepdims=False), SPACE, side)
     chip = lax.all_gather(own, "core", axis=0, tiled=True)
     edge = lax.dynamic_slice_in_dim(chip, 2 * core, 4, 0)
-    neighbours = [[s, (s + 1) % 32] for s in range(1, 32, 2)]
-    far = lax.all_gather(edge, SPACE, axis=0, axis_index_groups=neighbours)
-    far = lax.dynamic_index_in_dim(far, core, 0, keepdims=False)
-    near = lax.all_gather(lax.dynamic_index_in_dim(far, 3 * (1 - core), 0, keepdims=False), "core", axis=0)
-    near = lax.dynamic_index_in_dim(near, 1 - core, 0, keepdims=False)
+    pairs = [(s, (s + 1) % 32) for s in range(1, 32, 2)]
+    far = lax.ppermute(edge, SPACE, pairs + [(b, a) for a, b in pairs])
+    chip = chip.astype(F32)
+    core = core.reshape(1)
+    plane = lambda n: jax.ShapeDtypeStruct((n, K, CELLS), F32)
+    inner = pl.pallas_call(
+        inner_kernel,
+        out_shape=[plane(2), plane(4), plane(2), plane(2), plane(2)],
+        in_specs=[SMEM] + [VMEM] * (2 + BLOCKS),
+        out_specs=[VMEM] * 5,
+        scratch_shapes=scratch(6, (8,)),
+        compiler_params=params(24),
+        cost_estimate=cost(12),
+        name="inner",
+    )(core, chip, beta, *coefs)
     blocks = pl.pallas_call(
-        steps_kernel,
+        outer_kernel,
         out_shape=jax.ShapeDtypeStruct((16, 3, 8, CELLS), F32),
-        in_specs=[SMEM] + [VMEM] * (4 + BLOCKS),
+        in_specs=[SMEM] + [VMEM] * (9 + BLOCKS),
         out_specs=VMEM,
-        scratch_shapes=[pltpu.VMEM((2048, 9 * CELLS), BF16), pltpu.VMEM((11, K + 16, CELLS), F32)],
-        compiler_params=params(32),
-        name="steps",
-    )(core.reshape(1), chip.astype(F32), far.astype(F32), near.astype(F32), beta, *coefs)
+        scratch_shapes=scratch(3, (16,)),
+        compiler_params=params(24),
+        cost_estimate=cost(12),
+        name="outer",
+    )(core, chip, far.astype(F32), near.astype(F32), *inner, beta, *coefs)
     blocks = lax.all_to_all(blocks.astype(F16), SECT, split_axis=0, concat_axis=0, tiled=True)
     return blocks.transpose(1, 2, 0, 3).reshape(density.shape).astype(F32) * 512.0
 

time: 61.5 us -> 64.9 us (1.055)
  the two profiles are of different devices: /device:TPU:1 before, /device:TPU:8 now
where the time goes in v2:
time: 64.9 us; the launch traced here: 64.5 us
  starting transfers between devices  23.7 us (37%)
  blocking collectives  14.8 us (23%)
  Pallas kernels  12.5 us (19%)
  waiting for transfers between devices  9.99 us (15%)
  other arithmetic  2.5 us (4%)
  local copies, waits for them, and re-layouts  0.9 us (1%)
    all_to_all x1, blocking collectives, on_device(): lax.all_to_all(blocks.astype(F16), SECT, split_axis=0, concat_axis=0, til...  12.9 us
    ppermute x1, starting transfers between devices, on_device(): lax.ppermute(lax.dynamic_index_in_dim(own, 2 * core, 0, keepdims=False),...  12.2 us
    all_to_all x1, starting transfers between devices, on_device(): lax.all_to_all(blocks, SECT, split_axis=0, concat_axis=0, tiled=True)  9.5 us
    pallas_call x1, Pallas kernels, on_device(): pl.pallas_call(outer_kernel, out_shape=jax.ShapeDtypeStruct((16, 3, 8, CE...  6.79 us
    all_to_all x1, waiting for transfers between devices, on_device(): lax.all_to_all(blocks, SECT, split_axis=0, concat_axis=0, tiled=True)  6.22 us
    pallas_call x1, Pallas kernels, on_device(): pl.pallas_call(inner_kernel, out_shape=[plane(2), plane(4), plane(2), pla...  5.05 us
    ppermute x1, waiting for transfers between devices, on_device(): far = lax.ppermute(edge, SPACE, pairs + [(b, a) for a, b in pairs])  3.77 us
    all_gather x1, blocking collectives, on_device(): chip = lax.all_gather(own, 'core', axis=0, tiled=True)  1.96 us
  transfers between devices with their start and end apart: 3, of which 2 were waited for; matrix products, arithmetic and copies ran while one was open for 1% of the time, Pallas kernels for 9%

profile of v2, /device:TPU:8, one launch (start us, length us, event | category | flops | bytes accessed | tf_op | source)
XLA Modules:
  0.0 64.5 jit_solution(16655451338075343872)
XLA Ops:
  0.0 0.9 %convert_bitcast_fusion = f16[3,8,16,128]{3,1,2,0:T(8,128)(2,1)S(1)} fusion(f32[3,8,2048]{2,1,0:T(8,128)} %param.5), kind=kLoop, calls=%fused_computation.5 | loop fusion | flops 49152 | bytes 294912
  1.0 0.7 %copy.15 = f16[16,3,8,128]{3,2,1,0:T(8,128)(2,1)} copy(f16[16,3,8,128]{3,0,2,1:T(8,128)(2,1)S(1)} %bitcast.29) | data formatting | bytes 196608 | tf_op jit(solution)/shard_map/convert_element_type | solution.py:181
  1.7 0.0 copy-start
  1.7 0.0 copy-start.1
  1.7 0.0 copy-start.2
  1.7 9.5 %all-to-all-start = ((f16[16,3,8,128]{3,2,1,0:T(8,128)(2,1)}), f16[16,3,8,128]{3,2,1,0:T(8,128)(2,1)S(1)}, u32[]{:S(2)}, u32[]{:S(2)}) async-start(f16[16,3,8,128]{3,2,1,0:T(8,128)(2,1)} %copy.15), calls=%async_computation | async-start | bytes 196608 | tf_op jit(solution)/shard_map/all_to_all | solution.py:182
  11.2 0.7 %fusion.1 = (f16[3,1,128]{2,0,1:T(4,128)(2,1)S(1)}, f16[3,1,128]{2,0,1:T(4,128)(2,1)S(1)}) fusion(f32[3,2048]{1,0:T(4,128)} %param.6, s32[]{:T(128)S(6)} %select_n.10), kind=kLoop, calls=%fused_computation.11 | loop fusion | flops 1920 | bytes 3076 | tf_op jit(solution)/shard_map/broadcast_in_dim | solution.py:187
  11.9 0.1 pad.3.clone
  12.0 0.0 copy-done
  12.0 0.0 copy-done.1
  12.0 0.0 copy-done.2
  12.0 0.7 %prepare.1 = (bf16[128,128]{1,0:T(8,128)(2,1)S(1)}, bf16[128,256]{1,0:T(8,128)(2,1)S(1)}, bf16[112,512]{1,0:T(8,128)(2,1)S(1)}, bf16[96,768]{1,0:T(8,128)(2,1)S(...) custom-call(f32[128,128]{1,0:T(8,128)S(1)} %copy-done, ...), custom_call_target="tpu_custom_call" | custom-call | tf_op jit(solution)/shard_map/prepare/pallas_call | solution.py:69
  12.7 6.2 %all-to-all-done = f16[16,3,8,128]{3,2,1,0:T(8,128)(2,1)S(1)} async-done(((f16[16,3,8,128]{3,2,1,0:T(8,128)(2,1)}), f16[16,3,8,128]{3,2,1,0:T(8,128)(2,1)S(1)}, u32[]{:S(2)}, u32[]{:S(2)}) %all-to-all-start) | async-done | bytes 98336 | tf_op jit(solution)/shard_map/all_to_all | solution.py:182
  18.9 0.1 maximum_maximum_fusion
  19.0 2.0 %all_gather.3 = f16[6,144,128]{2,1,0:T(8,128)(2,1)S(1)} all-gather(f16[3,144,128]{2,1,0:T(8,128)(2,1)S(1)} %maximum_maximum_fusion), channel_id=1, replica_groups=mesh['chip'=16,'core'=2,'zl'=2,'y'=8] {'core'}, dimensions={0}, use_global_device_ids=true | all-gather | bytes 331776 | tf_op jit(solution)/shard_map/all_gather | solution.py:190
  21.0 12.2 %collective-permute-start.1 = (f16[144,128]{1,0:T(8,128)(2,1)S(1)}, f16[144,128]{1,0:T(8,128)(2,1)S(1)}, u32[]{:S(2)}, u32[]{:S(2)}) collective-permute-start(f16[144,128]{1,0:T(8,128)(2,1)S(1)} %dynamic-slice_bitcast_fusion), channel_id=1, source_target_pairs={{32,0},{16,48},{64,32},{48,80},{96,64},{80,112},{128,96},{112,144}... | collective-permute-start | bytes 110600 | tf_op jit(solution)/shard_map/ppermute | solution.py:189
  33.3 1.9 %collective-permute-start = (f16[4,144,128]{2,1,0:T(8,128)(2,1)S(1)}, f16[4,144,128]{2,1,0:T(8,128)(2,1)S(1)}, u32[]{:S(2)}, u32[]{:S(2)}) collective-permute-start(f16[4,144,128]{2,1,0:T(8,128)(2,1)S(1)} %constant_dynamic-slice_fusion), channel_id=1, source_target_pairs={{16,32},{48,64},{80,96},{112,128},{144,160},{176,192},{208,224},{2... | collective-permute-start | bytes 442376 | tf_op jit(solution)/shard_map/ppermute | solution.py:193
  35.3 5.0 %inner.1 = (f32[2,128,128]{2,1,0:T(8,128)S(1)}, f32[4,128,128]{2,1,0:T(8,128)S(1)}, f32[2,128,128]{2,1,0:T(8,128)S(1)}, f32[2,128,128]{2,1,0:T(8,128)S(1)}, f32[2,128,128]{2,1,0:T(8,128)S(1)}) custom-call(s32[1]{0:T(128)} %bitcast.core_ref, f32[6,144,128]{2,1,0:T(8,128)S(1)} %convert_element_type.41.chip_ref, ...), custom_call_target="tpu_custom_call" | custom-call | flops 3623878656 | bytes 3000000 | tf_op jit(solution)/shard_map/inner/pallas_call | solution.py:197
  40.3 0.0 collective-permute-done.1
  40.3 3.8 %collective-permute-done = f16[4,144,128]{2,1,0:T(8,128)(2,1)S(1)} collective-permute-done((f16[4,144,128]{2,1,0:T(8,128)(2,1)S(1)}, f16[4,144,128]{2,1,0:T(8,128)(2,1)S(1)}, u32[]{:S(2)}, u32[]{:S(2)}) %collective-permute-start) | collective-permute-done | bytes 147488 | tf_op jit(solution)/shard_map/ppermute | solution.py:193
  44.1 6.8 %outer.1 = f32[16,3,8,128]{3,2,1,0:T(8,128)S(1)} custom-call(s32[1]{0:T(128)} %bitcast.core_ref, f32[6,144,128]{2,1,0:T(8,128)S(1)} %convert_element_type.41.chip_ref, f32[4,144,128]{2,1,0:T(8,128)S(1)} %convert_element_type.42.far_ref, f32[144,128]{1,0:T(8,128)S(1)} %convert_element_type.43.near_ref, f32[2,128,128]{2,1,0:T(8,128)S(1)} %get-tuple-element.28.react1_ref, ...), custom_call_target="tpu_custom_call" | custom-call | flops 3623878656 | bytes 3000000 | tf_op jit(solution)/shard_map/outer/pallas_call | solution.py:207
  51.0 12.9 %all_to_all.10 = f16[16,3,8,128]{3,2,1,0:T(8,128)(2,1)S(1)} all-to-all(f16[16,3,8,128]{3,2,1,0:T(8,128)(2,1)S(1)} %convert_element_type.44), channel_id=1, replica_groups=mesh['chip'=16,'core'=2,'zl'=2,'y'=8] {'zl','y'}, dimensions={0} | all-to-all | bytes 196608 | tf_op jit(solution)/shard_map/all_to_all | solution.py:217
  63.8 0.7 %copy_bitcast_fusion = f32[3,8,2048]{2,1,0:T(8,128)} fusion(f16[16,3,8,128]{3,2,1,0:T(8,128)(2,1)S(1)} %all_to_all.10), kind=kLoop, calls=%fused_computation | loop fusion | flops 98304 | bytes 294912 | tf_op jit(solution)/shard_map/mul | solution.py:218
  (11 shorter events, 0.2 us)
Async XLA Ops:
  1.7 10.3 %copy-start = (f32[128,128]{1,0:T(8,128)S(1)}, f32[128,128]{1,0:T(8,128)}, u32[]{:S(2)}) copy-start(f32[128,128]{1,0:T(8,128)} %kernel_ref.1) | copy-start | bytes 196612
  1.7 10.3 %copy-start.1 = (f32[128,128]{1,0:T(8,128)S(1)}, f32[128,128]{1,0:T(8,128)}, u32[]{:S(2)}) copy-start(f32[128,128]{1,0:T(8,128)} %split_ref.1) | copy-start | bytes 196612
  1.7 10.3 %copy-start.2 = (s32[128,128]{1,0:T(8,128)S(1)}, s32[128,128]{1,0:T(8,128)}, u32[]{:S(2)}) copy-start(s32[128,128]{1,0:T(8,128)} %target_ref.1) | copy-start | bytes 196612
  1.7 17.2 %all-to-all-start = ((f16[16,3,8,128]{3,2,1,0:T(8,128)(2,1)}), f16[16,3,8,128]{3,2,1,0:T(8,128)(2,1)S(1)}, u32[]{:S(2)}, u32[]{:S(2)}) async-start(f16[16,3,8,128]{3,2,1,0:T(8,128)(2,1)} %copy.15), calls=%async_computation | async-start | bytes 196608 | tf_op jit(solution)/shard_map/all_to_all | solution.py:182
  21.0 19.3 %collective-permute-start.1 = (f16[144,128]{1,0:T(8,128)(2,1)S(1)}, f16[144,128]{1,0:T(8,128)(2,1)S(1)}, u32[]{:S(2)}, u32[]{:S(2)}) collective-permute-start(f16[144,128]{1,0:T(8,128)(2,1)S(1)} %dynamic-slice_bitcast_fusion), channel_id=1, source_target_pairs={{32,0},{16,48},{64,32},{48,80},{96,64},{80,112},{128,96},{112,144}... | collective-permute-start | bytes 110600 | tf_op jit(solution)/shard_map/ppermute | solution.py:189
  33.3 10.8 %collective-permute-start = (f16[4,144,128]{2,1,0:T(8,128)(2,1)S(1)}, f16[4,144,128]{2,1,0:T(8,128)(2,1)S(1)}, u32[]{:S(2)}, u32[]{:S(2)}) collective-permute-start(f16[4,144,128]{2,1,0:T(8,128)(2,1)S(1)} %constant_dynamic-slice_fusion), channel_id=1, source_target_pairs={{16,32},{48,64},{80,96},{112,128},{144,160},{176,192},{208,224},{2... | collective-permute-start | bytes 442376 | tf_op jit(solution)/shard_map/ppermute | solution.py:193

commit v3 on v2

--- a/solution.py
+++ b/solution.py
@@ -10,6 +10,8 @@
 CELLS = 128
 BLOCKS = 8
 B = 16
+START = [K * b * (b + 1) for b in range(BLOCKS + 1)]
+PAIRS = START[BLOCKS]
 SECT = ("zl", "y")
 SPACE = ("chip", "core")
 STEPS = 4
@@ -24,8 +26,8 @@
     return pltpu.CompilerParams(vmem_limit_bytes=mib * 1024 * 1024)
 
 
-def prepare_kernel(kernel_ref, split_ref, target_ref, beta_ref, *coef_refs):
-    kernel, split = kernel_ref[...], split_ref[...]
+def prepare_kernel(table_ref, beta_ref, coef_ref):
+    kernel, split = table_ref[:K], table_ref[K : 2 * K]
     beta = 0.5 * (kernel + kernel.T)
     weight = 0.5 * (split + split.T)
     beta_ref[...] = beta.astype(BF16)
@@ -34,7 +36,7 @@
     count = jnp.where(cols < rows, 2.0, jnp.where(cols == rows, 1.0, 0.0))
     low = 0.5 * beta * weight * count
     high = 0.5 * beta * (1.0 - weight) * count
-    target = jnp.where(cols <= rows, target_ref[...], 0)
+    target = jnp.where(cols <= rows, table_ref[2 * K :], 0.0).astype(jnp.int32)
     for block in range(BLOCKS):
         n = B * (block + 1)
         tiles = n * B // K
@@ -60,42 +62,39 @@
         for tile in range(tiles):
             a, b, t = (parts[which][tile] for which in range(3))
             value = jnp.where(ks == t, a, jnp.where(ks == t + 1, b, 0.0))
-            coef_refs[block][:, tile * K : (tile + 1) * K] = value.astype(BF16)
+            at = START[block] + tile * K
+            coef_ref[K - top :, at : at + K] = value.astype(BF16)
+            if block:
+                coef_ref[: K - top, at : at + K] = jnp.zeros((K - top, K), BF16)
 
 
 def prepare(kernel, split, target):
-    shapes = [jax.ShapeDtypeStruct((K, K), BF16)]
-    shapes += [jax.ShapeDtypeStruct((K - B * b, B * B * (b + 1)), BF16) for b in range(BLOCKS)]
+    shapes = [jax.ShapeDtypeStruct((K, K), BF16), jax.ShapeDtypeStruct((K, PAIRS), BF16)]
     return pl.pallas_call(
         prepare_kernel,
         out_shape=shapes,
-        in_specs=[VMEM] * 3,
-        out_specs=[VMEM] * (BLOCKS + 1),
+        in_specs=[VMEM],
+        out_specs=[VMEM] * 2,
         compiler_params=params(16),
         name="prepare",
-    )(kernel, split, target)
-
-
-def reaction(planes, beta, coefs, pair_ref):
+    )(jnp.concatenate([kernel, split, target.astype(F32)]))
+
+
+def reaction(planes, beta, coef, pair_ref):
     x = jnp.concatenate(planes, axis=1) if len(planes) > 1 else planes[0]
     width = x.shape[1]
     low = x.astype(BF16)
-    total = None
     for block in range(BLOCKS):
         n = B * (block + 1)
         for jj in range(B):
             j = B * block + jj
             factor = jnp.broadcast_to(x[j : j + 1], (B, width)).astype(BF16)
             for part in range(block + 1):
-                at = jj * n + B * part
+                at = START[block] + jj * n + B * part
                 pair_ref[at : at + B, :width] = low[B * part : B * (part + 1)] * factor
-        gain = jnp.dot(coefs[block][...], pair_ref[: B * n, :width], preferred_element_type=F32)
-        if block == 0:
-            total = gain
-        else:
-            total = jnp.concatenate([total[: B * block], total[B * block :] + gain], axis=0)
+    gain = jnp.dot(coef[...], pair_ref[:, :width], preferred_element_type=F32)
     rate = jnp.dot(beta[...], low, preferred_element_type=F32)
-    change = total - x * rate
+    change = gain - x * rate
     return [change[:, CELLS * p : CELLS * (p + 1)] for p in range(len(planes))]
 
 
@@ -105,31 +104,29 @@
     return here - (out - came)
 
 
-def inner_kernel(core_ref, chip_ref, beta_ref, *refs):
-    coefs, outs, (pair_ref, speed_ref) = refs[:BLOCKS], refs[BLOCKS:-2], refs[-2:]
-    react1_ref, state1_ref, react2_ref, state2_ref, react3_ref = outs
+def inner_kernel(core_ref, chip_ref, beta_ref, coef_ref, *refs):
+    react1_ref, state1_ref, react2_ref, state2_ref, react3_ref, pair_ref, speed_ref = refs
     core = core_ref[0]
     sign = (1 - 2 * core).astype(F32)
     planes = [chip_ref[5 * core + (1 - 2 * core) * p, :K] for p in range(6)]
     for p in range(6):
         speed_ref[p : p + 1] = chip_ref[p, K : K + 1] + chip_ref[p, K + 1 : K + 2] * (1.0 / 2048.0)
     faces = [sign * speed_ref[pl.ds(4 * core + (1 - 2 * core) * f, 1)] for f in range(5)]
-    changes = reaction(planes, beta_ref, coefs, pair_ref)
+    changes = reaction(planes, beta_ref, coef_ref, pair_ref)
     react1_ref[0], react1_ref[1] = changes[0], changes[5]
     planes = [moved(*planes[p - 1 : p + 2], faces[p - 1], faces[p]) + changes[p] for p in range(1, 5)]
     for p in range(4):
         state1_ref[p] = planes[p]
-    changes = reaction(planes, beta_ref, coefs, pair_ref)
+    changes = reaction(planes, beta_ref, coef_ref, pair_ref)
     react2_ref[0], react2_ref[1] = changes[0], changes[3]
     planes = [moved(*planes[p - 1 : p + 2], faces[p], faces[p + 1]) + changes[p] for p in range(1, 3)]
-    changes = reaction(planes, beta_ref, coefs, pair_ref)
+    changes = reaction(planes, beta_ref, coef_ref, pair_ref)
     for p in range(2):
         state2_ref[p] = planes[p]
         react3_ref[p] = changes[p]
 
 
-def outer_kernel(core_ref, chip_ref, far_ref, near_ref, react1_ref, state1_ref, react2_ref, state2_ref, react3_ref, beta_ref, *refs):
-    coefs, out_ref, pair_ref, speed_ref = refs[:BLOCKS], refs[BLOCKS], refs[BLOCKS + 1], refs[BLOCKS + 2]
+def outer_kernel(core_ref, chip_ref, far_ref, near_ref, react1_ref, state1_ref, react2_ref, state2_ref, react3_ref, beta_ref, coef_ref, out_ref, pair_ref, speed_ref):
     core = core_ref[0]
     step = 1 - 2 * core
     sign = step.astype(F32)
@@ -154,7 +151,7 @@
     known_states = [{5 + p: state1_ref[p] for p in range(4)}, {6 + p: state2_ref[p] for p in range(2)}, {}, {}]
     for t in range(STEPS):
         reacting = range(t + 1, t + 4)
-        change = dict(zip(reacting, reaction([state[w] for w in reacting], beta_ref, coefs, pair_ref)))
+        change = dict(zip(reacting, reaction([state[w] for w in reacting], beta_ref, coef_ref, pair_ref)))
         change.update(known_changes[t])
         after = dict(known_states[t])
         for w in range(t + 1, 10 - t):
@@ -168,7 +165,7 @@
 
 
 def scratch(planes, rows):
-    return [pltpu.VMEM((2048, planes * CELLS), BF16)] + [pltpu.VMEM((r, CELLS), F32) for r in rows]
+    return [pltpu.VMEM((PAIRS, planes * CELLS), BF16)] + [pltpu.VMEM((r, CELLS), F32) for r in rows]
 
 
 def cost(planes):
@@ -177,43 +174,43 @@
 
 def on_device(density, velocity, kernel, split, target):
     core = lax.axis_index("core").astype(jnp.int32)
-    beta, *coefs = prepare(kernel, split, target)
-    blocks = density.reshape(3, 8, 16, CELLS).transpose(2, 0, 1, 3).astype(F16)
-    blocks = lax.all_to_all(blocks, SECT, split_axis=0, concat_axis=0, tiled=True)
+    beta, coef = prepare(kernel, split, target)
+    blocks = density.reshape(3, 8, 16, CELLS).astype(F16)
+    blocks = lax.all_to_all(blocks, SECT, split_axis=2, concat_axis=2, tiled=True)
     speed = lax.dynamic_slice_in_dim(velocity, lax.axis_index(SECT) * CELLS, CELLS, 1)
     high = speed.astype(F16)
     rest = ((speed - high.astype(F32)) * 2048.0).astype(F16)
-    own = blocks.transpose(1, 0, 2, 3).reshape(3, K, CELLS)
+    own = blocks.transpose(0, 2, 1, 3).reshape(3, K, CELLS)
     own = jnp.concatenate([own, high[:, None], rest[:, None], jnp.zeros((3, 14, CELLS), F16)], axis=1)
-    side = [((s + 2) % 32, s) if s % 2 == 0 else (s, (s + 2) % 32) for s in range(32)]
-    near = lax.ppermute(lax.dynamic_index_in_dim(own, 2 * core, 0, keepdims=False), SPACE, side)
     chip = lax.all_gather(own, "core", axis=0, tiled=True)
     edge = lax.dynamic_slice_in_dim(chip, 2 * core, 4, 0)
     pairs = [(s, (s + 1) % 32) for s in range(1, 32, 2)]
     far = lax.ppermute(edge, SPACE, pairs + [(b, a) for a, b in pairs])
+    near = lax.all_gather(lax.dynamic_index_in_dim(far, 3 * (1 - core), 0, keepdims=False), "core", axis=0)
+    near = lax.dynamic_index_in_dim(near, 1 - core, 0, keepdims=False)
     chip = chip.astype(F32)
     core = core.reshape(1)
     plane = lambda n: jax.ShapeDtypeStruct((n, K, CELLS), F32)
     inner = pl.pallas_call(
         inner_kernel,
         out_shape=[plane(2), plane(4), plane(2), plane(2), plane(2)],
-        in_specs=[SMEM] + [VMEM] * (2 + BLOCKS),
+        in_specs=[SMEM] + [VMEM] * 3,
         out_specs=[VMEM] * 5,
         scratch_shapes=scratch(6, (8,)),
         compiler_params=params(24),
         cost_estimate=cost(12),
         name="inner",
-    )(core, chip, beta, *coefs)
+    )(core, chip, beta, coef)
     blocks = pl.pallas_call(
         outer_kernel,
         out_shape=jax.ShapeDtypeStruct((16, 3, 8, CELLS), F32),
-        in_specs=[SMEM] + [VMEM] * (9 + BLOCKS),
+        in_specs=[SMEM] + [VMEM] * 10,
         out_specs=VMEM,
         scratch_shapes=scratch(3, (16,)),
         compiler_params=params(24),
         cost_estimate=cost(12),
         name="outer",
-    )(core, chip, far.astype(F32), near.astype(F32), *inner, beta, *coefs)
+    )(core, chip, far.astype(F32), near.astype(F32), *inner, beta, coef)
     blocks = lax.all_to_all(blocks.astype(F16), SECT, split_axis=0, concat_axis=0, tiled=True)
     return blocks.transpose(1, 2, 0, 3).reshape(density.shape).astype(F32) * 512.0
 

time: 64.9 us -> 59.3 us (0.914)
  the two profiles are of different devices: /device:TPU:8 before, /device:TPU:1 now
where the time goes in v3:
time: 59.3 us; the launch traced here: 58.9 us
  blocking collectives  21.6 us (36%)
  starting transfers between devices  15.6 us (26%)
  Pallas kernels  12.6 us (21%)
  other arithmetic  4.87 us (8%)
  waiting for transfers between devices  4.02 us (7%)
    all_to_all x1, blocking collectives, on_device(): lax.all_to_all(blocks.astype(F16), SECT, split_axis=0, concat_axis=0, til...  9.98 us
    all_to_all x1, starting transfers between devices, on_device(): lax.all_to_all(blocks, SECT, split_axis=2, concat_axis=2, tiled=True)  9.56 us
    all_gather x1, blocking collectives, on_device(): lax.all_gather(lax.dynamic_index_in_dim(far, 3 * (1 - core), 0, keepdims=...  7.98 us
    pallas_call x1, Pallas kernels, on_device(): pl.pallas_call(outer_kernel, out_shape=jax.ShapeDtypeStruct((16, 3, 8, CE...  6.18 us
    ppermute x1, starting transfers between devices, on_device(): far = lax.ppermute(edge, SPACE, pairs + [(b, a) for a, b in pairs])  6.05 us
    pallas_call x1, Pallas kernels, on_device(): pl.pallas_call(inner_kernel, out_shape=[plane(2), plane(4), plane(2), pla...  5.45 us
    all_to_all x1, waiting for transfers between devices, on_device(): lax.all_to_all(blocks, SECT, split_axis=2, concat_axis=2, tiled=True)  4.02 us
    all_gather x1, blocking collectives, on_device(): chip = lax.all_gather(own, 'core', axis=0, tiled=True)  3.62 us
  transfers between devices with their start and end apart: 2, of which 1 were waited for; matrix products, arithmetic and copies ran while one was open for 4% of the time, Pallas kernels for 11%

profile of v3, /device:TPU:1, one launch (start us, length us, event | category | flops | bytes accessed | tf_op | source)
XLA Modules:
  0.0 58.9 jit_solution(15858260817807848820)
XLA Ops:
  0.0 1.6 %copy_bitcast_fusion.1 = f16[3,8,16,128]{3,1,0,2:T(8,128)(2,1)} fusion(f32[3,8,2048]{2,1,0:T(8,128)} %param.5), kind=kLoop, calls=%fused_computation.4 | loop fusion | flops 49152 | bytes 294912 | tf_op jit(solution)/shard_map/convert_element_type | solution.py:178
  1.6 9.6 %all-to-all-start = ((f16[3,8,16,128]{3,1,0,2:T(8,128)(2,1)}), f16[3,8,16,128]{3,1,0,2:T(8,128)(2,1)S(1)}, u32[]{:S(2)}, u32[]{:S(2)}) async-start(f16[3,8,16,128]{3,1,0,2:T(8,128)(2,1)} %copy_bitcast_fusion.1), calls=%async_computation | async-start | bytes 196608 | tf_op jit(solution)/shard_map/all_to_all | solution.py:179
  11.2 0.7 %fusion.1 = (f16[3,1,128]{2,0,1:T(4,128)(2,1)S(1)}, f16[3,1,128]{2,0,1:T(4,128)(2,1)S(1)}) fusion(f32[3,2048]{1,0:T(4,128)} %param.6, s32[]{:T(128)S(6)} %select_n.14), kind=kLoop, calls=%fused_computation.13 | loop fusion | flops 1920 | bytes 3076 | tf_op jit(solution)/shard_map/broadcast_in_dim | solution.py:184
  11.9 0.8 %convert_element_type.46 = f32[128,128]{1,0:T(8,128)S(1)} convert(s32[128,128]{1,0:T(8,128)} %param.9) | non-fusion elementwise | flops 16384 | bytes 131072 | tf_op jit(solution)/shard_map/convert_element_type | solution.py:80
  12.7 0.9 %pad_maximum_fusion.table_ref = f32[384,128]{1,0:T(8,128)S(1)} fusion(f32[128,128]{1,0:T(8,128)S(1)} %convert_element_type.46, f32[128,128]{1,0:T(8,128)} %param.8, f32[128,128]{1,0:T(8,128)} %param.7), kind=kLoop, calls=%fused_computation.1 | loop fusion | flops 98304 | bytes 393216 | tf_op jit(solution)/shard_map/concatenate | solution.py:80
  13.6 0.9 %prepare.1 = (bf16[128,128]{1,0:T(8,128)(2,1)S(1)}, bf16[128,9216]{1,0:T(8,128)(2,1)S(1)}) custom-call(f32[384,128]{1,0:T(8,128)S(1)} %pad_maximum_fusion.table_ref), custom_call_target="tpu_custom_call" | custom-call | tf_op jit(solution)/shard_map/prepare/pallas_call | solution.py:73
  14.6 0.1 pad.6.clone
  14.6 4.0 %all-to-all-done = f16[3,8,16,128]{3,1,0,2:T(8,128)(2,1)S(1)} async-done(((f16[3,8,16,128]{3,1,0,2:T(8,128)(2,1)}), f16[3,8,16,128]{3,1,0,2:T(8,128)(2,1)S(1)}, u32[]{:S(2)}, u32[]{:S(2)}) %all-to-all-start) | async-done | bytes 98336 | tf_op jit(solution)/shard_map/all_to_all | solution.py:179
  18.7 0.1 maximum_maximum_fusion
  18.8 3.6 %all_gather.7 = f16[6,144,128]{2,1,0:T(8,128)(2,1)S(1)} all-gather(f16[3,144,128]{2,1,0:T(8,128)(2,1)S(1)} %maximum_maximum_fusion), channel_id=1, replica_groups=mesh['chip'=16,'core'=2,'zl'=2,'y'=8] {'core'}, dimensions={0}, use_global_device_ids=true | all-gather | bytes 331776 | tf_op jit(solution)/shard_map/all_gather | solution.py:185
  22.5 6.1 %collective-permute-start = (f16[4,144,128]{2,1,0:T(8,128)(2,1)S(1)}, f16[4,144,128]{2,1,0:T(8,128)(2,1)S(1)}, u32[]{:S(2)}, u32[]{:S(2)}) collective-permute-start(f16[4,144,128]{2,1,0:T(8,128)(2,1)S(1)} %constant_dynamic-slice_fusion.1), channel_id=1, source_target_pairs={{16,32},{48,64},{80,96},{112,128},{144,160},{176,192},{208,224},{2... | collective-permute-start | bytes 442376 | tf_op jit(solution)/shard_map/ppermute | solution.py:188
  28.5 5.5 %inner.1 = (f32[2,128,128]{2,1,0:T(8,128)S(1)}, f32[4,128,128]{2,1,0:T(8,128)S(1)}, f32[2,128,128]{2,1,0:T(8,128)S(1)}, f32[2,128,128]{2,1,0:T(8,128)S(1)}, f32[2,128,128]{2,1,0:T(8,128)S(1)}) custom-call(s32[1]{0:T(128)} %bitcast.core_ref, f32[6,144,128]{2,1,0:T(8,128)S(1)} %convert_element_type.42.chip_ref, ...), custom_call_target="tpu_custom_call" | custom-call | flops 3623878656 | bytes 3000000 | tf_op jit(solution)/shard_map/inner/pallas_call | solution.py:194
  34.0 0.0 collective-permute-done
  34.0 8.0 %all_gather.8 = f16[2,144,128]{2,1,0:T(8,128)(2,1)S(1)} all-gather(f16[1,144,128]{2,1,0:T(8,128)(2,1)S(1)} %constant_dynamic-slice_fusion), channel_id=1, replica_groups=mesh['chip'=16,'core'=2,'zl'=2,'y'=8] {'core'}, dimensions={0}, use_global_device_ids=true | all-gather | bytes 110592 | tf_op jit(solution)/shard_map/all_gather | solution.py:189
  42.0 6.2 %outer.1 = f32[16,3,8,128]{3,2,1,0:T(8,128)S(1)} custom-call(s32[1]{0:T(128)} %bitcast.core_ref, f32[6,144,128]{2,1,0:T(8,128)S(1)} %convert_element_type.42.chip_ref, f32[4,144,128]{2,1,0:T(8,128)S(1)} %convert_element_type.43.far_ref, f32[144,128]{1,0:T(8,128)S(1)} %bitcast_convert_fusion.near_ref, f32[2,128,128]{2,1,0:T(8,128)S(1)} %get-tuple-element.14.react1_ref, ...), custom_call_target="tpu_custom_call" | custom-call | flops 3623878656 | bytes 3000000 | tf_op jit(solution)/shard_map/outer/pallas_call | solution.py:204
  48.3 10.0 %all_to_all.10 = f16[16,3,8,128]{3,2,1,0:T(8,128)(2,1)S(1)} all-to-all(f16[16,3,8,128]{3,2,1,0:T(8,128)(2,1)S(1)} %convert_element_type.47), channel_id=1, replica_groups=mesh['chip'=16,'core'=2,'zl'=2,'y'=8] {'zl','y'}, dimensions={0} | all-to-all | bytes 196608 | tf_op jit(solution)/shard_map/all_to_all | solution.py:214
  58.2 0.7 %copy_bitcast_fusion = f32[3,8,2048]{2,1,0:T(8,128)} fusion(f16[16,3,8,128]{3,2,1,0:T(8,128)(2,1)S(1)} %all_to_all.10), kind=kLoop, calls=%fused_computation | loop fusion | flops 98304 | bytes 294912 | tf_op jit(solution)/shard_map/mul | solution.py:215
  (10 shorter events, 0.2 us)
Async XLA Ops:
  1.6 17.1 %all-to-all-start = ((f16[3,8,16,128]{3,1,0,2:T(8,128)(2,1)}), f16[3,8,16,128]{3,1,0,2:T(8,128)(2,1)S(1)}, u32[]{:S(2)}, u32[]{:S(2)}) async-start(f16[3,8,16,128]{3,1,0,2:T(8,128)(2,1)} %copy_bitcast_fusion.1), calls=%async_computation | async-start | bytes 196608 | tf_op jit(solution)/shard_map/all_to_all | solution.py:179
  22.5 11.5 %collective-permute-start = (f16[4,144,128]{2,1,0:T(8,128)(2,1)S(1)}, f16[4,144,128]{2,1,0:T(8,128)(2,1)S(1)}, u32[]{:S(2)}, u32[]{:S(2)}) collective-permute-start(f16[4,144,128]{2,1,0:T(8,128)(2,1)S(1)} %constant_dynamic-slice_fusion.1), channel_id=1, source_target_pairs={{16,32},{48,64},{80,96},{112,128},{144,160},{176,192},{208,224},{2... | collective-permute-start | bytes 442376 | tf_op jit(solution)/shard_map/ppermute | solution.py:188

commit v4 on v3

--- a/solution.py
+++ b/solution.py
@@ -1,3 +1,5 @@
+import functools
+
 import jax
 import jax.numpy as jnp
 from jax import lax
@@ -84,15 +86,19 @@
     x = jnp.concatenate(planes, axis=1) if len(planes) > 1 else planes[0]
     width = x.shape[1]
     low = x.astype(BF16)
-    for block in range(BLOCKS):
-        n = B * (block + 1)
-        for jj in range(B):
-            j = B * block + jj
-            factor = jnp.broadcast_to(x[j : j + 1], (B, width)).astype(BF16)
-            for part in range(block + 1):
-                at = START[block] + jj * n + B * part
-                pair_ref[at : at + B, :width] = low[B * part : B * (part + 1)] * factor
-    gain = jnp.dot(coef[...], pair_ref[:, :width], preferred_element_type=F32)
+    gain = None
+    for group in ((range(4), range(4, 6), range(6, 8)) if len(planes) == 3 else (range(BLOCKS),)):
+        for block in group:
+            n = B * (block + 1)
+            for jj in range(B):
+                j = B * block + jj
+                factor = jnp.broadcast_to(x[j : j + 1], (B, width)).astype(BF16)
+                for part in range(block + 1):
+                    at = START[block] + jj * n + B * part
+                    pair_ref[at : at + B, :width] = low[B * part : B * (part + 1)] * factor
+        first, begin, end = B * group[0], START[group[0]], START[group[-1] + 1]
+        some = jnp.dot(coef[first:, begin:end], pair_ref[begin:end, :width], preferred_element_type=F32)
+        gain = some if gain is None else jnp.concatenate([gain[:first], gain[first:] + some], axis=0)
     rate = jnp.dot(beta[...], low, preferred_element_type=F32)
     change = gain - x * rate
     return [change[:, CELLS * p : CELLS * (p + 1)] for p in range(len(planes))]
@@ -104,9 +110,13 @@
     return here - (out - came)
 
 
-def inner_kernel(core_ref, chip_ref, beta_ref, coef_ref, *refs):
-    react1_ref, state1_ref, react2_ref, state2_ref, react3_ref, pair_ref, speed_ref = refs
-    core = core_ref[0]
+def inner_kernel(turn, place_ref, chip_ref, beta_ref, coef_ref, *refs):
+    @pl.when(place_ref[1] == turn)
+    def _():
+        inner(place_ref[0], chip_ref, beta_ref, coef_ref, *refs[-7:])
+
+
+def inner(core, chip_ref, beta_ref, coef_ref, react1_ref, state1_ref, react2_ref, state2_ref, react3_ref, pair_ref, speed_ref):
     sign = (1 - 2 * core).astype(F32)
     planes = [chip_ref[5 * core + (1 - 2 * core) * p, :K] for p in range(6)]
     for p in range(6):
@@ -126,8 +136,8 @@
         react3_ref[p] = changes[p]
 
 
-def outer_kernel(core_ref, chip_ref, far_ref, near_ref, react1_ref, state1_ref, react2_ref, state2_ref, react3_ref, beta_ref, coef_ref, out_ref, pair_ref, speed_ref):
-    core = core_ref[0]
+def outer_kernel(place_ref, chip_ref, far_ref, near_ref, react1_ref, state1_ref, react2_ref, state2_ref, react3_ref, beta_ref, coef_ref, out_ref, pair_ref, speed_ref):
+    core = place_ref[0]
     step = 1 - 2 * core
     sign = step.astype(F32)
 
@@ -172,6 +182,20 @@
     return pl.CostEstimate(flops=2 * K * 9216 * CELLS * planes, bytes_accessed=3000000, transcendentals=0)
 
 
+def react_inside(turn, place, chip, beta, coef, found):
+    return pl.pallas_call(
+        functools.partial(inner_kernel, turn),
+        out_shape=[jax.ShapeDtypeStruct((n, K, CELLS), F32) for n in (2, 4, 2, 2, 2)],
+        in_specs=[SMEM] + [VMEM] * (3 + len(found)),
+        out_specs=[VMEM] * 5,
+        scratch_shapes=scratch(6, (8,)),
+        input_output_aliases={4 + n: n for n in range(len(found))},
+        compiler_params=params(24),
+        cost_estimate=cost(12),
+        name=("before", "after")[turn],
+    )(place, chip, beta, coef, *found)
+
+
 def on_device(density, velocity, kernel, split, target):
     core = lax.axis_index("core").astype(jnp.int32)
     beta, coef = prepare(kernel, split, target)
@@ -183,24 +207,16 @@
     own = blocks.transpose(0, 2, 1, 3).reshape(3, K, CELLS)
     own = jnp.concatenate([own, high[:, None], rest[:, None], jnp.zeros((3, 14, CELLS), F16)], axis=1)
     chip = lax.all_gather(own, "core", axis=0, tiled=True)
+    place = jnp.stack([core, jnp.where(lax.axis_index("chip") % 4 < 2, 0, 1).astype(jnp.int32)])
+    wide = chip.astype(F32)
+    found = react_inside(0, place, wide, beta, coef, [])
     edge = lax.dynamic_slice_in_dim(chip, 2 * core, 4, 0)
+    side = lax.dynamic_index_in_dim(own, 2 * core, 0, keepdims=False)
+    edge, side, found = lax.optimization_barrier((edge, side, found))
     pairs = [(s, (s + 1) % 32) for s in range(1, 32, 2)]
     far = lax.ppermute(edge, SPACE, pairs + [(b, a) for a, b in pairs])
-    near = lax.all_gather(lax.dynamic_index_in_dim(far, 3 * (1 - core), 0, keepdims=False), "core", axis=0)
-    near = lax.dynamic_index_in_dim(near, 1 - core, 0, keepdims=False)
-    chip = chip.astype(F32)
-    core = core.reshape(1)
-    plane = lambda n: jax.ShapeDtypeStruct((n, K, CELLS), F32)
-    inner = pl.pallas_call(
-        inner_kernel,
-        out_shape=[plane(2), plane(4), plane(2), plane(2), plane(2)],
-        in_specs=[SMEM] + [VMEM] * 3,
-        out_specs=[VMEM] * 5,
-        scratch_shapes=scratch(6, (8,)),
-        compiler_params=params(24),
-        cost_estimate=cost(12),
-        name="inner",
-    )(core, chip, beta, coef)
+    near = lax.ppermute(side, SPACE, [((s + 2) % 32, s) if s % 2 == 0 else (s, (s + 2) % 32) for s in range(32)])
+    found = react_inside(1, place, wide, beta, coef, found)
     blocks = pl.pallas_call(
         outer_kernel,
         out_shape=jax.ShapeDtypeStruct((16, 3, 8, CELLS), F32),
@@ -210,7 +226,7 @@
         compiler_params=params(24),
         cost_estimate=cost(12),
         name="outer",
-    )(core, chip, far.astype(F32), near.astype(F32), *inner, beta, coef)
+    )(place, wide, far.astype(F32), near.astype(F32), *found, beta, coef)
     blocks = lax.all_to_all(blocks.astype(F16), SECT, split_axis=0, concat_axis=0, tiled=True)
     return blocks.transpose(1, 2, 0, 3).reshape(density.shape).astype(F32) * 512.0
 

time: 59.3 us -> 61.7 us (1.040)
  blocking collectives: 21.6 us -> 13.9 us
  waiting for transfers between devices: 4.02 us -> 10.2 us
  Pallas kernels: 12.6 us -> 14.5 us
  starting transfers between devices: 15.6 us -> 17.5 us
    all_gather x1 -> x0, blocking collectives: 7.98 us -> none  [on_device(): lax.all_gather(lax.dynamic_index_in_dim(far, 3 * (1 - core), 0, keepdims=...]
    ppermute x0 -> x1, waiting for transfers between devices: none -> 6.25 us  [on_device(): lax.ppermute(side, SPACE, [((s + 2) % 32, s) if s % 2 == 0 else (s, (s +...]
    ppermute x0 -> x1, starting transfers between devices: none -> 1.92 us  [on_device(): lax.ppermute(side, SPACE, [((s + 2) % 32, s) if s % 2 == 0 else (s, (s +...]
    pallas_call x1 -> x2, Pallas kernels: 5.45 us -> 6.69 us  [react_inside(): pl.pallas_call(functools.partial(inner_kernel, turn), out_shape=[jax.Shap...]
    pallas_call x1, Pallas kernels: 6.18 us -> 6.85 us  [on_device(): pl.pallas_call(outer_kernel, out_shape=jax.ShapeDtypeStruct((16, 3, 8, CE...]
  transfers between devices with their start and end apart: 2 -> 3, of which waited for: 1 -> 2; matrix products, arithmetic and copies ran while one was open for 4% -> 4% of each run, Pallas kernels for 11% -> 3%
where the time goes in v4:
time: 61.7 us; the launch traced here: 61.3 us
  starting transfers between devices  17.5 us (28%)
  Pallas kernels  14.5 us (24%)
  blocking collectives  13.9 us (23%)
  waiting for transfers between devices  10.2 us (17%)
  other arithmetic  4.95 us (8%)
    all_to_all x1, blocking collectives, on_device(): lax.all_to_all(blocks.astype(F16), SECT, split_axis=0, concat_axis=0, til...  10.2 us
    all_to_all x1, starting transfers between devices, on_device(): lax.all_to_all(blocks, SECT, split_axis=2, concat_axis=2, tiled=True)  9.56 us
    pallas_call x1, Pallas kernels, on_device(): pl.pallas_call(outer_kernel, out_shape=jax.ShapeDtypeStruct((16, 3, 8, CE...  6.85 us
    pallas_call x2, Pallas kernels, react_inside(): pl.pallas_call(functools.partial(inner_kernel, turn), out_shape=[jax.Shap...  6.69 us
    ppermute x1, waiting for transfers between devices, on_device(): lax.ppermute(side, SPACE, [((s + 2) % 32, s) if s % 2 == 0 else (s, (s +...  6.25 us
    ppermute x1, starting transfers between devices, on_device(): far = lax.ppermute(edge, SPACE, pairs + [(b, a) for a, b in pairs])  6.06 us
    all_to_all x1, waiting for transfers between devices, on_device(): lax.all_to_all(blocks, SECT, split_axis=2, concat_axis=2, tiled=True)  3.93 us
    all_gather x1, blocking collectives, on_device(): chip = lax.all_gather(own, 'core', axis=0, tiled=True)  3.62 us
  transfers between devices with their start and end apart: 3, of which 2 were waited for; matrix products, arithmetic and copies ran while one was open for 4% of the time, Pallas kernels for 3%

profile of v4, /device:TPU:1, one launch (start us, length us, event | category | flops | bytes accessed | tf_op | source)
XLA Modules:
  0.0 61.3 jit_solution(2792107633079378920)
XLA Ops:
  0.0 1.6 %copy_bitcast_fusion.1 = f16[3,8,16,128]{3,1,0,2:T(8,128)(2,1)} fusion(f32[3,8,2048]{2,1,0:T(8,128)} %param.5), kind=kLoop, calls=%fused_computation.4 | loop fusion | flops 49152 | bytes 294912 | tf_op jit(solution)/shard_map/convert_element_type | solution.py:202
  1.6 9.6 %all-to-all-start = ((f16[3,8,16,128]{3,1,0,2:T(8,128)(2,1)}), f16[3,8,16,128]{3,1,0,2:T(8,128)(2,1)S(1)}, u32[]{:S(2)}, u32[]{:S(2)}) async-start(f16[3,8,16,128]{3,1,0,2:T(8,128)(2,1)} %copy_bitcast_fusion.1), calls=%async_computation | async-start | bytes 196608 | tf_op jit(solution)/shard_map/all_to_all | solution.py:203
  11.2 0.7 %fusion.1 = (f16[3,1,128]{2,0,1:T(4,128)(2,1)S(1)}, f16[3,1,128]{2,0,1:T(4,128)(2,1)S(1)}) fusion(f32[3,2048]{1,0:T(4,128)} %param.6, s32[]{:T(128)S(6)} %select_n.23), kind=kLoop, calls=%fused_computation.13 | loop fusion | flops 1920 | bytes 3076 | tf_op jit(solution)/shard_map/broadcast_in_dim | solution.py:208
  11.9 0.8 %convert_element_type.41 = f32[128,128]{1,0:T(8,128)S(1)} convert(s32[128,128]{1,0:T(8,128)} %param.9) | non-fusion elementwise | flops 16384 | bytes 131072 | tf_op jit(solution)/shard_map/convert_element_type | solution.py:82
  12.7 0.9 %pad_maximum_fusion.table_ref = f32[384,128]{1,0:T(8,128)S(1)} fusion(f32[128,128]{1,0:T(8,128)S(1)} %convert_element_type.41, f32[128,128]{1,0:T(8,128)} %param.8, f32[128,128]{1,0:T(8,128)} %param.7), kind=kLoop, calls=%fused_computation.1 | loop fusion | flops 98304 | bytes 393216 | tf_op jit(solution)/shard_map/concatenate | solution.py:82
  13.6 0.9 %prepare.1 = (bf16[128,128]{1,0:T(8,128)(2,1)S(1)}, bf16[128,9216]{1,0:T(8,128)(2,1)S(1)}) custom-call(f32[384,128]{1,0:T(8,128)S(1)} %pad_maximum_fusion.table_ref), custom_call_target="tpu_custom_call" | custom-call | tf_op jit(solution)/shard_map/prepare/pallas_call | solution.py:75
  14.6 0.1 pad.6.clone
  14.6 0.1 pad_add_fusion.place_ref
  14.7 3.9 %all-to-all-done = f16[3,8,16,128]{3,1,0,2:T(8,128)(2,1)S(1)} async-done(((f16[3,8,16,128]{3,1,0,2:T(8,128)(2,1)}), f16[3,8,16,128]{3,1,0,2:T(8,128)(2,1)S(1)}, u32[]{:S(2)}, u32[]{:S(2)}) %all-to-all-start) | async-done | bytes 98336 | tf_op jit(solution)/shard_map/all_to_all | solution.py:203
  18.7 0.1 maximum_maximum_fusion
  18.8 3.6 %all_gather.3 = f16[6,144,128]{2,1,0:T(8,128)(2,1)S(1)} all-gather(f16[3,144,128]{2,1,0:T(8,128)(2,1)S(1)} %maximum_maximum_fusion), channel_id=1, replica_groups=mesh['chip'=16,'core'=2,'zl'=2,'y'=8] {'core'}, dimensions={0}, use_global_device_ids=true | all-gather | bytes 331776 | tf_op jit(solution)/shard_map/all_gather | solution.py:209
  22.5 6.0 %before.1 = (f32[2,128,128]{2,1,0:T(8,128)S(1)}, f32[4,128,128]{2,1,0:T(8,128)S(1)}, f32[2,128,128]{2,1,0:T(8,128)S(1)}, f32[2,128,128]{2,1,0:T(8,128)S(1)}, f32[2,128,128]{2,1,0:T(8,128)S(1)}) custom-call(s32[2]{0:T(128)S(1)} %pad_add_fusion.place_ref, f32[6,144,128]{2,1,0:T(8,128)S(1)} %convert_element_type.40.chip_ref, ...), custom_call_target="tpu_custom_call" | custom-call | flops 3623878656 | bytes 3000000 | tf_op jit(solution)/shard_map/before/pallas_call | solution.py:186
  28.5 6.1 %collective-permute-start = (f16[4,144,128]{2,1,0:T(8,128)(2,1)S(1)}, f16[4,144,128]{2,1,0:T(8,128)(2,1)S(1)}, u32[]{:S(2)}, u32[]{:S(2)}) collective-permute-start(f16[4,144,128]{2,1,0:T(8,128)(2,1)S(1)} %constant_dynamic-slice_fusion), channel_id=1, source_target_pairs={{16,32},{48,64},{80,96},{112,128},{144,160},{176,192},{208,224},{2... | collective-permute-start | bytes 442376 | tf_op jit(solution)/shard_map/ppermute | solution.py:217
  34.5 1.9 %collective-permute-start.1 = (f16[144,128]{1,0:T(8,128)(2,1)S(1)}, f16[144,128]{1,0:T(8,128)(2,1)S(1)}, u32[]{:S(2)}, u32[]{:S(2)}) collective-permute-start(f16[144,128]{1,0:T(8,128)(2,1)S(1)} %dynamic-slice_bitcast_fusion), channel_id=1, source_target_pairs={{32,0},{16,48},{64,32},{48,80},{96,64},{80,112},{128,96},{112,144}... | collective-permute-start | bytes 110600 | tf_op jit(solution)/shard_map/ppermute | solution.py:218
  36.5 0.7 %after.1 = (f32[2,128,128]{2,1,0:T(8,128)S(1)}, f32[4,128,128]{2,1,0:T(8,128)S(1)}, f32[2,128,128]{2,1,0:T(8,128)S(1)}, f32[2,128,128]{2,1,0:T(8,128)S(1)}, f32[2,128,128]{2,1,0:T(8,128)S(1)}) custom-call(s32[2]{0:T(128)S(1)} %pad_add_fusion.place_ref, ...), custom_call_target="tpu_custom_call", output_to_operand_aliasing={{0}: (4, {}), {1}: (5, {}), {2}: (6, {}), {3}: (7, {}), {4}... | custom-call | flops 3623878656 | bytes 3000000 | tf_op jit(solution)/shard_map/after/pallas_call | solution.py:186
  37.2 6.3 %collective-permute-done.1 = f16[144,128]{1,0:T(8,128)(2,1)S(1)} collective-permute-done((f16[144,128]{1,0:T(8,128)(2,1)S(1)}, f16[144,128]{1,0:T(8,128)(2,1)S(1)}, u32[]{:S(2)}, u32[]{:S(2)}) %collective-permute-start.1) | collective-permute-done | bytes 36896 | tf_op jit(solution)/shard_map/ppermute | solution.py:218
  43.5 0.0 collective-permute-done
  43.5 6.9 %outer.1 = f32[16,3,8,128]{3,2,1,0:T(8,128)S(1)} custom-call(s32[2]{0:T(128)S(1)} %pad_add_fusion.place_ref, f32[6,144,128]{2,1,0:T(8,128)S(1)} %convert_element_type.40.chip_ref, f32[4,144,128]{2,1,0:T(8,128)S(1)} %convert_element_type.42.far_ref, f32[144,128]{1,0:T(8,128)S(1)} %convert_element_type.43.near_ref, ...), custom_call_target="tpu_custom_call" | custom-call | flops 3623878656 | bytes 3000000 | tf_op jit(solution)/shard_map/outer/pallas_call | solution.py:220
  50.4 10.2 %all_to_all.10 = f16[16,3,8,128]{3,2,1,0:T(8,128)(2,1)S(1)} all-to-all(f16[16,3,8,128]{3,2,1,0:T(8,128)(2,1)S(1)} %convert_element_type.44), channel_id=1, replica_groups=mesh['chip'=16,'core'=2,'zl'=2,'y'=8] {'zl','y'}, dimensions={0} | all-to-all | bytes 196608 | tf_op jit(solution)/shard_map/all_to_all | solution.py:230
  60.6 0.7 %copy_bitcast_fusion = f32[3,8,2048]{2,1,0:T(8,128)} fusion(f16[16,3,8,128]{3,2,1,0:T(8,128)(2,1)S(1)} %all_to_all.10), kind=kLoop, calls=%fused_computation | loop fusion | flops 98304 | bytes 294912 | tf_op jit(solution)/shard_map/mul | solution.py:231
  (10 shorter events, 0.2 us)
Async XLA Ops:
  1.6 17.1 %all-to-all-start = ((f16[3,8,16,128]{3,1,0,2:T(8,128)(2,1)}), f16[3,8,16,128]{3,1,0,2:T(8,128)(2,1)S(1)}, u32[]{:S(2)}, u32[]{:S(2)}) async-start(f16[3,8,16,128]{3,1,0,2:T(8,128)(2,1)} %copy_bitcast_fusion.1), calls=%async_computation | async-start | bytes 196608 | tf_op jit(solution)/shard_map/all_to_all | solution.py:203
  28.5 15.0 %collective-permute-start = (f16[4,144,128]{2,1,0:T(8,128)(2,1)S(1)}, f16[4,144,128]{2,1,0:T(8,128)(2,1)S(1)}, u32[]{:S(2)}, u32[]{:S(2)}) collective-permute-start(f16[4,144,128]{2,1,0:T(8,128)(2,1)S(1)} %constant_dynamic-slice_fusion), channel_id=1, source_target_pairs={{16,32},{48,64},{80,96},{112,128},{144,160},{176,192},{208,224},{2... | collective-permute-start | bytes 442376 | tf_op jit(solution)/shard_map/ppermute | solution.py:217
  34.5 8.9 %collective-permute-start.1 = (f16[144,128]{1,0:T(8,128)(2,1)S(1)}, f16[144,128]{1,0:T(8,128)(2,1)S(1)}, u32[]{:S(2)}, u32[]{:S(2)}) collective-permute-start(f16[144,128]{1,0:T(8,128)(2,1)S(1)} %dynamic-slice_bitcast_fusion), channel_id=1, source_target_pairs={{32,0},{16,48},{64,32},{48,80},{96,64},{80,112},{128,96},{112,144}... | collective-permute-start | bytes 110600 | tf_op jit(solution)/shard_map/ppermute | solution.py:218

commit v5 on v3

--- a/solution.py
+++ b/solution.py
@@ -104,19 +104,37 @@
     return here - (out - came)
 
 
-def inner_kernel(core_ref, chip_ref, beta_ref, coef_ref, *refs):
-    react1_ref, state1_ref, react2_ref, state2_ref, react3_ref, pair_ref, speed_ref = refs
-    core = core_ref[0]
+def inner_faces(core, chip_ref, speed_ref):
     sign = (1 - 2 * core).astype(F32)
-    planes = [chip_ref[5 * core + (1 - 2 * core) * p, :K] for p in range(6)]
     for p in range(6):
         speed_ref[p : p + 1] = chip_ref[p, K : K + 1] + chip_ref[p, K + 1 : K + 2] * (1.0 / 2048.0)
-    faces = [sign * speed_ref[pl.ds(4 * core + (1 - 2 * core) * f, 1)] for f in range(5)]
+    return [sign * speed_ref[pl.ds(4 * core + (1 - 2 * core) * f, 1)] for f in range(5)]
+
+
+def inner_first(core, chip_ref, beta_ref, coef_ref, react1_ref, state1_ref, pair_ref, speed_ref):
+    faces = inner_faces(core, chip_ref, speed_ref)
+    planes = [chip_ref[5 * core + (1 - 2 * core) * p, :K] for p in range(6)]
     changes = reaction(planes, beta_ref, coef_ref, pair_ref)
     react1_ref[0], react1_ref[1] = changes[0], changes[5]
-    planes = [moved(*planes[p - 1 : p + 2], faces[p - 1], faces[p]) + changes[p] for p in range(1, 5)]
-    for p in range(4):
-        state1_ref[p] = planes[p]
+    for p in range(1, 5):
+        state1_ref[p - 1] = moved(*planes[p - 1 : p + 2], faces[p - 1], faces[p]) + changes[p]
+
+
+def before_kernel(place_ref, chip_ref, beta_ref, coef_ref, react1_ref, state1_ref, pair_ref, speed_ref):
+    @pl.when(place_ref[1] == 0)
+    def _():
+        inner_first(place_ref[0], chip_ref, beta_ref, coef_ref, react1_ref, state1_ref, pair_ref, speed_ref)
+
+
+def after_kernel(place_ref, chip_ref, beta_ref, coef_ref, _, __, react1_ref, state1_ref, react2_ref, state2_ref, react3_ref, pair_ref, speed_ref):
+    core = place_ref[0]
+
+    @pl.when(place_ref[1] == 1)
+    def _():
+        inner_first(core, chip_ref, beta_ref, coef_ref, react1_ref, state1_ref, pair_ref, speed_ref)
+
+    faces = inner_faces(core, chip_ref, speed_ref)
+    planes = [state1_ref[p] for p in range(4)]
     changes = reaction(planes, beta_ref, coef_ref, pair_ref)
     react2_ref[0], react2_ref[1] = changes[0], changes[3]
     planes = [moved(*planes[p - 1 : p + 2], faces[p], faces[p + 1]) + changes[p] for p in range(1, 3)]
@@ -126,8 +144,8 @@
         react3_ref[p] = changes[p]
 
 
-def outer_kernel(core_ref, chip_ref, far_ref, near_ref, react1_ref, state1_ref, react2_ref, state2_ref, react3_ref, beta_ref, coef_ref, out_ref, pair_ref, speed_ref):
-    core = core_ref[0]
+def outer_kernel(place_ref, chip_ref, far_ref, near_ref, react1_ref, state1_ref, react2_ref, state2_ref, react3_ref, beta_ref, coef_ref, out_ref, pair_ref, speed_ref):
+    core = place_ref[0]
     step = 1 - 2 * core
     sign = step.astype(F32)
 
@@ -172,6 +190,20 @@
     return pl.CostEstimate(flops=2 * K * 9216 * CELLS * planes, bytes_accessed=3000000, transcendentals=0)
 
 
+def react_inside(kernel, place, chip, beta, coef, found, outs):
+    return pl.pallas_call(
+        kernel,
+        out_shape=[jax.ShapeDtypeStruct((n, K, CELLS), F32) for n in outs],
+        in_specs=[SMEM] + [VMEM] * (3 + len(found)),
+        out_specs=[VMEM] * len(outs),
+        scratch_shapes=scratch(6, (8,)),
+        input_output_aliases={4 + n: n for n in range(len(found))},
+        compiler_params=params(24),
+        cost_estimate=cost(6),
+        name=kernel.__name__.partition("_")[0],
+    )(place, chip, beta, coef, *found)
+
+
 def on_device(density, velocity, kernel, split, target):
     core = lax.axis_index("core").astype(jnp.int32)
     beta, coef = prepare(kernel, split, target)
@@ -183,24 +215,16 @@
     own = blocks.transpose(0, 2, 1, 3).reshape(3, K, CELLS)
     own = jnp.concatenate([own, high[:, None], rest[:, None], jnp.zeros((3, 14, CELLS), F16)], axis=1)
     chip = lax.all_gather(own, "core", axis=0, tiled=True)
+    place = jnp.stack([core, jnp.where(lax.axis_index("chip") % 4 < 2, 0, 1).astype(jnp.int32)])
+    wide = chip.astype(F32)
+    found = react_inside(before_kernel, place, wide, beta, coef, [], (2, 4))
     edge = lax.dynamic_slice_in_dim(chip, 2 * core, 4, 0)
+    edge, found = lax.optimization_barrier((edge, found))
     pairs = [(s, (s + 1) % 32) for s in range(1, 32, 2)]
     far = lax.ppermute(edge, SPACE, pairs + [(b, a) for a, b in pairs])
+    found = react_inside(after_kernel, place, wide, beta, coef, found, (2, 4, 2, 2, 2))
     near = lax.all_gather(lax.dynamic_index_in_dim(far, 3 * (1 - core), 0, keepdims=False), "core", axis=0)
     near = lax.dynamic_index_in_dim(near, 1 - core, 0, keepdims=False)
-    chip = chip.astype(F32)
-    core = core.reshape(1)
-    plane = lambda n: jax.ShapeDtypeStruct((n, K, CELLS), F32)
-    inner = pl.pallas_call(
-        inner_kernel,
-        out_shape=[plane(2), plane(4), plane(2), plane(2), plane(2)],
-        in_specs=[SMEM] + [VMEM] * 3,
-        out_specs=[VMEM] * 5,
-        scratch_shapes=scratch(6, (8,)),
-        compiler_params=params(24),
-        cost_estimate=cost(12),
-        name="inner",
-    )(core, chip, beta, coef)
     blocks = pl.pallas_call(
         outer_kernel,
         out_shape=jax.ShapeDtypeStruct((16, 3, 8, CELLS), F32),
@@ -210,7 +234,7 @@
         compiler_params=params(24),
         cost_estimate=cost(12),
         name="outer",
-    )(core, chip, far.astype(F32), near.astype(F32), *inner, beta, coef)
+    )(place, wide, far.astype(F32), near.astype(F32), *found, beta, coef)
     blocks = lax.all_to_all(blocks.astype(F16), SECT, split_axis=0, concat_axis=0, tiled=True)
     return blocks.transpose(1, 2, 0, 3).reshape(density.shape).astype(F32) * 512.0
 

time: 59.3 us -> 59.4 us (level)
  blocking collectives: 21.6 us -> 19.5 us
  Pallas kernels: 12.6 us -> 14.2 us
    all_gather x1, blocking collectives: 7.98 us -> 5.76 us  [on_device(): lax.all_gather(lax.dynamic_index_in_dim(far, 3 * (1 - core), 0, keepdims=...]
    pallas_call x1 -> x2, Pallas kernels: 5.45 us -> 6.54 us  [react_inside(): pl.pallas_call(kernel, out_shape=[jax.ShapeDtypeStruct((n, K, CELLS), F32...]
  transfers between devices with their start and end apart: 2 -> 2, of which waited for: 1 -> 2; matrix products, arithmetic and copies ran while one was open for 4% -> 4% of each run, Pallas kernels for 11% -> 8%
where the time goes in v5:
time: 59.4 us; the launch traced here: 59 us
  blocking collectives  19.5 us (33%)
  starting transfers between devices  15.6 us (26%)
  Pallas kernels  14.2 us (24%)
  other arithmetic  4.95 us (8%)
  waiting for transfers between devices  4.42 us (7%)
    all_to_all x1, blocking collectives, on_device(): lax.all_to_all(blocks.astype(F16), SECT, split_axis=0, concat_axis=0, til...  10.2 us
    all_to_all x1, starting transfers between devices, on_device(): lax.all_to_all(blocks, SECT, split_axis=2, concat_axis=2, tiled=True)  9.56 us
    pallas_call x1, Pallas kernels, on_device(): pl.pallas_call(outer_kernel, out_shape=jax.ShapeDtypeStruct((16, 3, 8, CE...  6.73 us
    pallas_call x2, Pallas kernels, react_inside(): pl.pallas_call(kernel, out_shape=[jax.ShapeDtypeStruct((n, K, CELLS), F32...  6.54 us
    ppermute x1, starting transfers between devices, on_device(): far = lax.ppermute(edge, SPACE, pairs + [(b, a) for a, b in pairs])  6.05 us
    all_gather x1, blocking collectives, on_device(): lax.all_gather(lax.dynamic_index_in_dim(far, 3 * (1 - core), 0, keepdims=...  5.76 us
    all_to_all x1, waiting for transfers between devices, on_device(): lax.all_to_all(blocks, SECT, split_axis=2, concat_axis=2, tiled=True)  3.93 us
    all_gather x1, blocking collectives, on_device(): chip = lax.all_gather(own, 'core', axis=0, tiled=True)  3.62 us
  transfers between devices with their start and end apart: 2, of which 2 were waited for; matrix products, arithmetic and copies ran while one was open for 4% of the time, Pallas kernels for 8%

profile of v5, /device:TPU:1, one launch (start us, length us, event | category | flops | bytes accessed | tf_op | source)
XLA Modules:
  0.0 59.0 jit_solution(18330127593133534920)
XLA Ops:
  0.0 1.6 %copy_bitcast_fusion.1 = f16[3,8,16,128]{3,1,0,2:T(8,128)(2,1)} fusion(f32[3,8,2048]{2,1,0:T(8,128)} %param.5), kind=kLoop, calls=%fused_computation.4 | loop fusion | flops 49152 | bytes 294912 | tf_op jit(solution)/shard_map/convert_element_type | solution.py:210
  1.6 9.6 %all-to-all-start = ((f16[3,8,16,128]{3,1,0,2:T(8,128)(2,1)}), f16[3,8,16,128]{3,1,0,2:T(8,128)(2,1)S(1)}, u32[]{:S(2)}, u32[]{:S(2)}) async-start(f16[3,8,16,128]{3,1,0,2:T(8,128)(2,1)} %copy_bitcast_fusion.1), calls=%async_computation | async-start | bytes 196608 | tf_op jit(solution)/shard_map/all_to_all | solution.py:211
  11.2 0.7 %fusion.1 = (f16[3,1,128]{2,0,1:T(4,128)(2,1)S(1)}, f16[3,1,128]{2,0,1:T(4,128)(2,1)S(1)}) fusion(f32[3,2048]{1,0:T(4,128)} %param.6, s32[]{:T(128)S(6)} %select_n.27), kind=kLoop, calls=%fused_computation.14 | loop fusion | flops 1920 | bytes 3076 | tf_op jit(solution)/shard_map/broadcast_in_dim | solution.py:216
  11.9 0.8 %convert_element_type.43 = f32[128,128]{1,0:T(8,128)S(1)} convert(s32[128,128]{1,0:T(8,128)} %param.9) | non-fusion elementwise | flops 16384 | bytes 131072 | tf_op jit(solution)/shard_map/convert_element_type | solution.py:80
  12.7 0.9 %pad_maximum_fusion.table_ref = f32[384,128]{1,0:T(8,128)S(1)} fusion(f32[128,128]{1,0:T(8,128)S(1)} %convert_element_type.43, f32[128,128]{1,0:T(8,128)} %param.8, f32[128,128]{1,0:T(8,128)} %param.7), kind=kLoop, calls=%fused_computation.1 | loop fusion | flops 98304 | bytes 393216 | tf_op jit(solution)/shard_map/concatenate | solution.py:80
  13.6 0.9 %prepare.1 = (bf16[128,128]{1,0:T(8,128)(2,1)S(1)}, bf16[128,9216]{1,0:T(8,128)(2,1)S(1)}) custom-call(f32[384,128]{1,0:T(8,128)S(1)} %pad_maximum_fusion.table_ref), custom_call_target="tpu_custom_call" | custom-call | tf_op jit(solution)/shard_map/prepare/pallas_call | solution.py:73
  14.6 0.1 pad.6.clone
  14.6 0.1 pad_add_fusion.place_ref
  14.7 3.9 %all-to-all-done = f16[3,8,16,128]{3,1,0,2:T(8,128)(2,1)S(1)} async-done(((f16[3,8,16,128]{3,1,0,2:T(8,128)(2,1)}), f16[3,8,16,128]{3,1,0,2:T(8,128)(2,1)S(1)}, u32[]{:S(2)}, u32[]{:S(2)}) %all-to-all-start) | async-done | bytes 98336 | tf_op jit(solution)/shard_map/all_to_all | solution.py:211
  18.7 0.1 maximum_maximum_fusion
  18.8 3.6 %all_gather.7 = f16[6,144,128]{2,1,0:T(8,128)(2,1)S(1)} all-gather(f16[3,144,128]{2,1,0:T(8,128)(2,1)S(1)} %maximum_maximum_fusion), channel_id=1, replica_groups=mesh['chip'=16,'core'=2,'zl'=2,'y'=8] {'core'}, dimensions={0}, use_global_device_ids=true | all-gather | bytes 331776 | tf_op jit(solution)/shard_map/all_gather | solution.py:217
  22.5 2.6 %before.1 = (f32[2,128,128]{2,1,0:T(8,128)S(1)}, f32[4,128,128]{2,1,0:T(8,128)S(1)}) custom-call(s32[2]{0:T(128)S(1)} %pad_add_fusion.place_ref, f32[6,144,128]{2,1,0:T(8,128)S(1)} %convert_element_type.42.chip_ref, bf16[128,128]{1,0:T(8,128)(2,1)S(1)} %get-tuple-element.17.beta_ref, bf16[128,9216]{1,0:T(8,128)(2,1)S(1)} %get-tuple-element.18.coef_ref), custom_call_target="tpu_custom_call" | custom-call | flops 1811939328 | bytes 3000000 | tf_op jit(solution)/shard_map/before/pallas_call | solution.py:194
  25.1 6.0 %collective-permute-start = (f16[4,144,128]{2,1,0:T(8,128)(2,1)S(1)}, f16[4,144,128]{2,1,0:T(8,128)(2,1)S(1)}, u32[]{:S(2)}, u32[]{:S(2)}) collective-permute-start(f16[4,144,128]{2,1,0:T(8,128)(2,1)S(1)} %constant_dynamic-slice_fusion.1), channel_id=1, source_target_pairs={{16,32},{48,64},{80,96},{112,128},{144,160},{176,192},{208,224},{2... | collective-permute-start | bytes 442376 | tf_op jit(solution)/shard_map/ppermute | solution.py:224
  31.2 3.9 %after.1 = (f32[2,128,128]{2,1,0:T(8,128)S(1)}, f32[4,128,128]{2,1,0:T(8,128)S(1)}, f32[2,128,128]{2,1,0:T(8,128)S(1)}, f32[2,128,128]{2,1,0:T(8,128)S(1)}, f32[2,128,128]{2,1,0:T(8,128)S(1)}) custom-call(s32[2]{0:T(128)S(1)} %pad_add_fusion.place_ref, ...), custom_call_target="tpu_custom_call", output_to_operand_aliasing={{0}: (4, {}), {1}: (5, {})} | custom-call | flops 1811939328 | bytes 3000000 | tf_op jit(solution)/shard_map/after/pallas_call | solution.py:194
  35.1 0.5 collective-permute-done
  35.6 5.8 %all_gather.8 = f16[2,144,128]{2,1,0:T(8,128)(2,1)S(1)} all-gather(f16[1,144,128]{2,1,0:T(8,128)(2,1)S(1)} %constant_dynamic-slice_fusion), channel_id=1, replica_groups=mesh['chip'=16,'core'=2,'zl'=2,'y'=8] {'core'}, dimensions={0}, use_global_device_ids=true | all-gather | bytes 110592 | tf_op jit(solution)/shard_map/all_gather | solution.py:226
  41.4 6.7 %outer.1 = f32[16,3,8,128]{3,2,1,0:T(8,128)S(1)} custom-call(s32[2]{0:T(128)S(1)} %pad_add_fusion.place_ref, f32[6,144,128]{2,1,0:T(8,128)S(1)} %convert_element_type.42.chip_ref, f32[4,144,128]{2,1,0:T(8,128)S(1)} %convert_element_type.44.far_ref, f32[144,128]{1,0:T(8,128)S(1)} %bitcast_convert_fusion.near_ref, ...), custom_call_target="tpu_custom_call" | custom-call | flops 3623878656 | bytes 3000000 | tf_op jit(solution)/shard_map/outer/pallas_call | solution.py:228
  48.1 10.2 %all_to_all.10 = f16[16,3,8,128]{3,2,1,0:T(8,128)(2,1)S(1)} all-to-all(f16[16,3,8,128]{3,2,1,0:T(8,128)(2,1)S(1)} %convert_element_type.47), channel_id=1, replica_groups=mesh['chip'=16,'core'=2,'zl'=2,'y'=8] {'zl','y'}, dimensions={0} | all-to-all | bytes 196608 | tf_op jit(solution)/shard_map/all_to_all | solution.py:238
  58.3 0.7 %copy_bitcast_fusion = f32[3,8,2048]{2,1,0:T(8,128)} fusion(f16[16,3,8,128]{3,2,1,0:T(8,128)(2,1)S(1)} %all_to_all.10), kind=kLoop, calls=%fused_computation | loop fusion | flops 98304 | bytes 294912 | tf_op jit(solution)/shard_map/mul | solution.py:239
  (10 shorter events, 0.2 us)
Async XLA Ops:
  1.6 17.1 %all-to-all-start = ((f16[3,8,16,128]{3,1,0,2:T(8,128)(2,1)}), f16[3,8,16,128]{3,1,0,2:T(8,128)(2,1)S(1)}, u32[]{:S(2)}, u32[]{:S(2)}) async-start(f16[3,8,16,128]{3,1,0,2:T(8,128)(2,1)} %copy_bitcast_fusion.1), calls=%async_computation | async-start | bytes 196608 | tf_op jit(solution)/shard_map/all_to_all | solution.py:211
  25.1 10.4 %collective-permute-start = (f16[4,144,128]{2,1,0:T(8,128)(2,1)S(1)}, f16[4,144,128]{2,1,0:T(8,128)(2,1)S(1)}, u32[]{:S(2)}, u32[]{:S(2)}) collective-permute-start(f16[4,144,128]{2,1,0:T(8,128)(2,1)S(1)} %constant_dynamic-slice_fusion.1), channel_id=1, source_target_pairs={{16,32},{48,64},{80,96},{112,128},{144,160},{176,192},{208,224},{2... | collective-permute-start | bytes 442376 | tf_op jit(solution)/shard_map/ppermute | solution.py:224

commit v6 on v4

--- a/solution.py
+++ b/solution.py
@@ -1,5 +1,3 @@
-import functools
-
 import jax
 import jax.numpy as jnp
 from jax import lax
@@ -87,7 +85,7 @@
     width = x.shape[1]
     low = x.astype(BF16)
     gain = None
-    for group in ((range(4), range(4, 6), range(6, 8)) if len(planes) == 3 else (range(BLOCKS),)):
+    for group in [range(BLOCKS)] if len(planes) > 3 else [[block] for block in range(BLOCKS)]:
         for block in group:
             n = B * (block + 1)
             for jj in range(B):
@@ -110,18 +108,17 @@
     return here - (out - came)
 
 
-def inner_kernel(turn, place_ref, chip_ref, beta_ref, coef_ref, *refs):
-    @pl.when(place_ref[1] == turn)
-    def _():
-        inner(place_ref[0], chip_ref, beta_ref, coef_ref, *refs[-7:])
-
-
-def inner(core, chip_ref, beta_ref, coef_ref, react1_ref, state1_ref, react2_ref, state2_ref, react3_ref, pair_ref, speed_ref):
+def inner_faces(core, chip_ref, speed_ref):
     sign = (1 - 2 * core).astype(F32)
-    planes = [chip_ref[5 * core + (1 - 2 * core) * p, :K] for p in range(6)]
     for p in range(6):
         speed_ref[p : p + 1] = chip_ref[p, K : K + 1] + chip_ref[p, K + 1 : K + 2] * (1.0 / 2048.0)
-    faces = [sign * speed_ref[pl.ds(4 * core + (1 - 2 * core) * f, 1)] for f in range(5)]
+    return [sign * speed_ref[pl.ds(4 * core + (1 - 2 * core) * f, 1)] for f in range(5)]
+
+
+def inner(core, chip_ref, beta_ref, coef_ref, found, pair_ref, speed_ref):
+    react1_ref, state1_ref, react2_ref, state2_ref, react3_ref = found
+    faces = inner_faces(core, chip_ref, speed_ref)
+    planes = [chip_ref[5 * core + (1 - 2 * core) * p, :K] for p in range(6)]
     changes = reaction(planes, beta_ref, coef_ref, pair_ref)
     react1_ref[0], react1_ref[1] = changes[0], changes[5]
     planes = [moved(*planes[p - 1 : p + 2], faces[p - 1], faces[p]) + changes[p] for p in range(1, 5)]
@@ -136,40 +133,69 @@
         react3_ref[p] = changes[p]
 
 
-def outer_kernel(place_ref, chip_ref, far_ref, near_ref, react1_ref, state1_ref, react2_ref, state2_ref, react3_ref, beta_ref, coef_ref, out_ref, pair_ref, speed_ref):
+def before_kernel(place_ref, chip_ref, beta_ref, coef_ref, *refs):
+    @pl.when(place_ref[1] == 0)
+    def _():
+        inner(place_ref[0], chip_ref, beta_ref, coef_ref, refs[:5], refs[5], refs[6])
+
+
+def outer_kernel(place_ref, chip_ref, beta_ref, coef_ref, far_ref, near_ref, *refs):
+    out_ref, found = refs[5], refs[6:11]
+    pair_ref, speed_ref, state_ref, change_ref = refs[11:]
+    react1_ref, state1_ref, react2_ref, state2_ref, react3_ref = found
     core = place_ref[0]
     step = 1 - 2 * core
     sign = step.astype(F32)
 
+    @pl.when(place_ref[1] == 1)
+    def _():
+        inner(core, chip_ref, beta_ref, coef_ref, found, pair_ref, speed_ref)
+
     def speed(ref, p):
         return ref[p, K : K + 1] + ref[p, K + 1 : K + 2] * (1.0 / 2048.0)
 
     for p in range(4):
         speed_ref[p : p + 1] = speed(far_ref, 3 * core + step * p)
+        state_ref[0, p] = far_ref[3 * core + step * p, :K]
     for p in range(6):
         speed_ref[4 + p : 5 + p] = speed(chip_ref, 5 * core + step * p)
+        state_ref[0, 4 + p] = chip_ref[5 * core + step * p, :K]
     speed_ref[10:11] = near_ref[K : K + 1] + near_ref[K + 1 : K + 2] * (1.0 / 2048.0)
-    faces = [sign * speed_ref[pl.ds(core + f, 1)] for f in range(10)]
-
-    def advanced(state, change, w):
-        return moved(state[w - 1], state[w], state[w + 1], faces[w - 1], faces[w]) + change[w]
-
-    state = {w: far_ref[3 * core + step * w, :K] for w in range(4)}
-    state.update({4 + p: chip_ref[5 * core + step * p, :K] for p in range(6)})
-    state[10] = near_ref[:K]
-    known_changes = [{4: react1_ref[0], 9: react1_ref[1]}, {5: react2_ref[0], 8: react2_ref[1]}, {6: react3_ref[0], 7: react3_ref[1]}, {}]
-    known_states = [{5 + p: state1_ref[p] for p in range(4)}, {6 + p: state2_ref[p] for p in range(2)}, {}, {}]
-    for t in range(STEPS):
-        reacting = range(t + 1, t + 4)
-        change = dict(zip(reacting, reaction([state[w] for w in reacting], beta_ref, coef_ref, pair_ref)))
-        change.update(known_changes[t])
-        after = dict(known_states[t])
+    state_ref[0, 10] = near_ref[:K]
+
+    known_changes = [
+        {4: (react1_ref, 0), 9: (react1_ref, 1)},
+        {5: (react2_ref, 0), 8: (react2_ref, 1)},
+        {6: (react3_ref, 0), 7: (react3_ref, 1)},
+        {},
+    ]
+    known_states = [{5 + p: (state1_ref, p) for p in range(4)}, {6 + p: (state2_ref, p) for p in range(2)}, {}, {}]
+
+    def transport(t):
+        now, later = t % 2, (t + 1) % 2
+        faces = [sign * speed_ref[pl.ds(core + f, 1)] for f in range(10)]
+        change = {t + 1 + p: (change_ref, p) for p in range(3)} | known_changes[t]
         for w in range(t + 1, 10 - t):
-            if w not in after:
-                after[w] = advanced(state, change, w)
-        state = after
+            if w in known_states[t]:
+                ref, at = known_states[t][w]
+                state_ref[later, w] = ref[at]
+            else:
+                ref, at = change[w]
+                near = [state_ref[now, v] for v in (w - 1, w, w + 1)]
+                state_ref[later, w] = moved(*near, faces[w - 1], faces[w]) + ref[at]
+
+    def advance(t, _):
+        half = lax.rem(t, 2)
+        planes = [state_ref[half, t + 1 + p] for p in range(3)]
+        for p, change in enumerate(reaction(planes, beta_ref, coef_ref, pair_ref)):
+            change_ref[p] = change
+        for at in range(STEPS):
+            pl.when(t == at)(lambda at=at: transport(at))
+        return 0
+
+    lax.fori_loop(0, STEPS, advance, 0)
     for p in range(3):
-        value = state[4 + p] * (1.0 / 512.0)
+        value = state_ref[STEPS % 2, 4 + p] * (1.0 / 512.0)
         for d in range(16):
             out_ref[d, 2 * core + step * p] = value[8 * d : 8 * d + 8]
 
@@ -180,20 +206,6 @@
 
 def cost(planes):
     return pl.CostEstimate(flops=2 * K * 9216 * CELLS * planes, bytes_accessed=3000000, transcendentals=0)
-
-
-def react_inside(turn, place, chip, beta, coef, found):
-    return pl.pallas_call(
-        functools.partial(inner_kernel, turn),
-        out_shape=[jax.ShapeDtypeStruct((n, K, CELLS), F32) for n in (2, 4, 2, 2, 2)],
-        in_specs=[SMEM] + [VMEM] * (3 + len(found)),
-        out_specs=[VMEM] * 5,
-        scratch_shapes=scratch(6, (8,)),
-        input_output_aliases={4 + n: n for n in range(len(found))},
-        compiler_params=params(24),
-        cost_estimate=cost(12),
-        name=("before", "after")[turn],
-    )(place, chip, beta, coef, *found)
 
 
 def on_device(density, velocity, kernel, split, target):
@@ -209,24 +221,35 @@
     chip = lax.all_gather(own, "core", axis=0, tiled=True)
     place = jnp.stack([core, jnp.where(lax.axis_index("chip") % 4 < 2, 0, 1).astype(jnp.int32)])
     wide = chip.astype(F32)
-    found = react_inside(0, place, wide, beta, coef, [])
-    edge = lax.dynamic_slice_in_dim(chip, 2 * core, 4, 0)
-    side = lax.dynamic_index_in_dim(own, 2 * core, 0, keepdims=False)
-    edge, side, found = lax.optimization_barrier((edge, side, found))
-    pairs = [(s, (s + 1) % 32) for s in range(1, 32, 2)]
-    far = lax.ppermute(edge, SPACE, pairs + [(b, a) for a, b in pairs])
-    near = lax.ppermute(side, SPACE, [((s + 2) % 32, s) if s % 2 == 0 else (s, (s + 2) % 32) for s in range(32)])
-    found = react_inside(1, place, wide, beta, coef, found)
-    blocks = pl.pallas_call(
-        outer_kernel,
-        out_shape=jax.ShapeDtypeStruct((16, 3, 8, CELLS), F32),
-        in_specs=[SMEM] + [VMEM] * 10,
-        out_specs=VMEM,
-        scratch_shapes=scratch(3, (16,)),
+    shapes = [jax.ShapeDtypeStruct((n, K, CELLS), F32) for n in (2, 4, 2, 2, 2)]
+    found = pl.pallas_call(
+        before_kernel,
+        out_shape=shapes,
+        in_specs=[SMEM] + [VMEM] * 3,
+        out_specs=[VMEM] * 5,
+        scratch_shapes=scratch(6, (8,)),
         compiler_params=params(24),
         cost_estimate=cost(12),
+        name="before",
+    )(place, wide, beta, coef)
+    edge = lax.dynamic_slice_in_dim(chip, 2 * core, 4, 0)
+    edge, found = lax.optimization_barrier((edge, found))
+    neighbours = [[s, (s + 1) % 32] for s in range(1, 32, 2)]
+    far = lax.all_gather(edge, SPACE, axis=0, axis_index_groups=neighbours)
+    far = lax.dynamic_index_in_dim(far, core, 0, keepdims=False)
+    near = lax.all_gather(lax.dynamic_index_in_dim(far, 3 * (1 - core), 0, keepdims=False), "core", axis=0)
+    near = lax.dynamic_index_in_dim(near, 1 - core, 0, keepdims=False)
+    blocks, *_ = pl.pallas_call(
+        outer_kernel,
+        out_shape=[jax.ShapeDtypeStruct((16, 3, 8, CELLS), F32), *shapes],
+        in_specs=[SMEM] + [VMEM] * 10,
+        out_specs=[VMEM] * 6,
+        scratch_shapes=scratch(6, (16,)) + [pltpu.VMEM((2, 11, K, CELLS), F32), pltpu.VMEM((3, K, CELLS), F32)],
+        input_output_aliases={6 + n: 1 + n for n in range(5)},
+        compiler_params=params(32),
+        cost_estimate=cost(12),
         name="outer",
-    )(place, wide, far.astype(F32), near.astype(F32), *found, beta, coef)
+    )(place, wide, beta, coef, far.astype(F32), near.astype(F32), *found)
     blocks = lax.all_to_all(blocks.astype(F16), SECT, split_axis=0, concat_axis=0, tiled=True)
     return blocks.transpose(1, 2, 0, 3).reshape(density.shape).astype(F32) * 512.0
 

time: 61.7 us -> 58.6 us (0.950)
  blocking collectives: 13.9 us -> 26.7 us
  starting transfers between devices: 17.5 us -> 9.56 us
  waiting for transfers between devices: 10.2 us -> 3.92 us
  Pallas kernels: 14.5 us -> 12.8 us
    all_gather x0 -> x2, blocking collectives: none -> 12.1 us  [the longest x1 9.56 us: on_device(): far = lax.all_gather(edge, SPACE, axis=0, axis_index_groups=neighbours)]
    ppermute x2 -> x0, starting transfers between devices: 7.98 us -> none  [the longest x1 6.06 us: on_device(): far = lax.ppermute(edge, SPACE, pairs + [(b, a) for a, b in pairs])]
    ppermute x2 -> x0, waiting for transfers between devices: 6.26 us -> none  [the longest x1 6.25 us: on_device(): lax.ppermute(side, SPACE, [((s + 2) % 32, s) if s % 2 == 0 else (s, (s +...]
    pallas_call x3 -> x2, Pallas kernels: 13.5 us -> 11.9 us  [the longest x1 6.03 us: on_device(): pl.pallas_call(outer_kernel, out_shape=[jax.ShapeDtypeStruct((16, 3, 8, C...]
    all_to_all x1, blocking collectives: 10.2 us -> 11 us  [on_device(): lax.all_to_all(blocks.astype(F16), SECT, split_axis=0, concat_axis=0, til...]
  transfers between devices with their start and end apart: 3 -> 1, of which waited for: 2 -> 1; matrix products, arithmetic and copies ran while one was open for 4% -> 4% of each run, Pallas kernels for 3% -> 2%
where the time goes in v6:
time: 58.6 us; the launch traced here: 58.2 us
  blocking collectives  26.7 us (46%)
  Pallas kernels  12.8 us (22%)
  starting transfers between devices  9.56 us (16%)
  other arithmetic  4.95 us (8%)
  waiting for transfers between devices  3.92 us (7%)
    all_to_all x1, blocking collectives, on_device(): lax.all_to_all(blocks.astype(F16), SECT, split_axis=0, concat_axis=0, til...  11 us
    all_to_all x1, starting transfers between devices, on_device(): lax.all_to_all(blocks, SECT, split_axis=2, concat_axis=2, tiled=True)  9.56 us
    all_gather x1, blocking collectives, on_device(): far = lax.all_gather(edge, SPACE, axis=0, axis_index_groups=neighbours)  9.56 us
    pallas_call x1, Pallas kernels, on_device(): pl.pallas_call(outer_kernel, out_shape=[jax.ShapeDtypeStruct((16, 3, 8, C...  6.03 us
    pallas_call x1, Pallas kernels, on_device(): pl.pallas_call(before_kernel, out_shape=shapes, in_specs=[SMEM] + [VMEM]...  5.87 us
    all_to_all x1, waiting for transfers between devices, on_device(): lax.all_to_all(blocks, SECT, split_axis=2, concat_axis=2, tiled=True)  3.92 us
    all_gather x1, blocking collectives, on_device(): chip = lax.all_gather(own, 'core', axis=0, tiled=True)  3.62 us
    all_gather x1, blocking collectives, on_device(): lax.all_gather(lax.dynamic_index_in_dim(far, 3 * (1 - core), 0, keepdims=...  2.53 us
  transfers between devices with their start and end apart: 1, of which 1 were waited for; matrix products, arithmetic and copies ran while one was open for 4% of the time, Pallas kernels for 2%

profile of v6, /device:TPU:1, one launch (start us, length us, event | category | flops | bytes accessed | tf_op | source)
XLA Modules:
  0.0 58.2 jit_solution(12589287471331245660)
XLA Ops:
  0.0 1.6 %copy_bitcast_fusion.1 = f16[3,8,16,128]{3,1,0,2:T(8,128)(2,1)} fusion(f32[3,8,2048]{2,1,0:T(8,128)} %param.5), kind=kLoop, calls=%fused_computation.5 | loop fusion | flops 49152 | bytes 294912 | tf_op jit(solution)/shard_map/convert_element_type | solution.py:214
  1.6 9.6 %all-to-all-start = ((f16[3,8,16,128]{3,1,0,2:T(8,128)(2,1)}), f16[3,8,16,128]{3,1,0,2:T(8,128)(2,1)S(1)}, u32[]{:S(2)}, u32[]{:S(2)}) async-start(f16[3,8,16,128]{3,1,0,2:T(8,128)(2,1)} %copy_bitcast_fusion.1), calls=%async_computation | async-start | bytes 196608 | tf_op jit(solution)/shard_map/all_to_all | solution.py:215
  11.2 0.7 %fusion.1 = (f16[3,1,128]{2,0,1:T(4,128)(2,1)S(1)}, f16[3,1,128]{2,0,1:T(4,128)(2,1)S(1)}) fusion(f32[3,2048]{1,0:T(4,128)} %param.6, s32[]{:T(128)S(6)} %select_n.35), kind=kLoop, calls=%fused_computation.15 | loop fusion | flops 1920 | bytes 3076 | tf_op jit(solution)/shard_map/broadcast_in_dim | solution.py:220
  11.9 0.8 %convert_element_type.45 = f32[128,128]{1,0:T(8,128)S(1)} convert(s32[128,128]{1,0:T(8,128)} %param.9) | non-fusion elementwise | flops 16384 | bytes 131072 | tf_op jit(solution)/shard_map/convert_element_type | solution.py:80
  12.7 0.9 %pad_maximum_fusion.table_ref = f32[384,128]{1,0:T(8,128)S(1)} fusion(f32[128,128]{1,0:T(8,128)S(1)} %convert_element_type.45, f32[128,128]{1,0:T(8,128)} %param.8, f32[128,128]{1,0:T(8,128)} %param.7), kind=kLoop, calls=%fused_computation.1 | loop fusion | flops 98304 | bytes 393216 | tf_op jit(solution)/shard_map/concatenate | solution.py:80
  13.6 0.9 %prepare.1 = (bf16[128,128]{1,0:T(8,128)(2,1)S(1)}, bf16[128,9216]{1,0:T(8,128)(2,1)S(1)}) custom-call(f32[384,128]{1,0:T(8,128)S(1)} %pad_maximum_fusion.table_ref), custom_call_target="tpu_custom_call" | custom-call | tf_op jit(solution)/shard_map/prepare/pallas_call | solution.py:73
  14.6 0.1 pad.6.clone
  14.7 0.1 pad_add_fusion.place_ref
  14.7 3.9 %all-to-all-done = f16[3,8,16,128]{3,1,0,2:T(8,128)(2,1)S(1)} async-done(((f16[3,8,16,128]{3,1,0,2:T(8,128)(2,1)}), f16[3,8,16,128]{3,1,0,2:T(8,128)(2,1)S(1)}, u32[]{:S(2)}, u32[]{:S(2)}) %all-to-all-start) | async-done | bytes 98336 | tf_op jit(solution)/shard_map/all_to_all | solution.py:215
  18.7 0.1 maximum_maximum_fusion
  18.8 3.6 %all_gather.13 = f16[6,144,128]{2,1,0:T(8,128)(2,1)S(1)} all-gather(f16[3,144,128]{2,1,0:T(8,128)(2,1)S(1)} %maximum_maximum_fusion), channel_id=1, replica_groups=mesh['chip'=16,'core'=2,'zl'=2,'y'=8] {'core'}, dimensions={0}, use_global_device_ids=true | all-gather | bytes 331776 | tf_op jit(solution)/shard_map/all_gather | solution.py:221
  22.5 5.9 %before.1 = (f32[2,128,128]{2,1,0:T(8,128)S(1)}, f32[4,128,128]{2,1,0:T(8,128)S(1)}, f32[2,128,128]{2,1,0:T(8,128)S(1)}, f32[2,128,128]{2,1,0:T(8,128)S(1)}, f32[2,128,128]{2,1,0:T(8,128)S(1)}) custom-call(s32[2]{0:T(128)S(1)} %pad_add_fusion.place_ref, f32[6,144,128]{2,1,0:T(8,128)S(1)} %convert_element_type.44.chip_ref, ...), custom_call_target="tpu_custom_call" | custom-call | flops 3623878656 | bytes 3000000 | tf_op jit(solution)/shard_map/before/pallas_call | solution.py:225
  28.3 9.6 %all-gather = f16[8,144,128]{2,1,0:T(8,128)(2,1)S(1)} all-gather(f16[4,144,128]{2,1,0:T(8,128)(2,1)S(1)} %constant_dynamic-slice_fusion.1), channel_id=2, replica_groups={{16,32},{48,64},{80,96},{112,128},{144,160},{176,192},{208,224},{240,25..., dimensions={0}, use_global_device_ids=true | all-gather | bytes 442368 | tf_op jit(solution)/shard_map/all_gather | solution.py:238
  38.0 2.5 %all-gather.1 = f16[2,1,144,128]{3,2,1,0:T(8,128)(2,1)S(1)} all-gather(f16[1,1,144,128]{3,2,1,0:T(8,128)(2,1)S(1)} %constant_dynamic-slice_fusion), channel_id=3, replica_groups=mesh['chip'=16,'core'=2,'zl'=2,'y'=8] {'core'}, dimensions={0}, use_global_device_ids=true | all-gather | bytes 110592 | tf_op jit(solution)/shard_map/all_gather | solution.py:240
  40.5 6.0 %outer.1 = (f32[16,3,8,128]{3,2,1,0:T(8,128)S(1)}, f32[2,128,128]{2,1,0:T(8,128)S(1)}, f32[4,128,128]{2,1,0:T(8,128)S(1)}, f32[2,128,128]{2,1,0:T(8,128)S(1)}, f...) custom-call(s32[2]{0:T(128)S(1)} %pad_add_fusion.place_ref, ...), custom_call_target="tpu_custom_call", output_to_operand_aliasing={{1}: (6, {}), {2}: (7, {}), {3}: (8, {}), {4}: (9, {}), {5}... | custom-call | flops 3623878656 | bytes 3000000 | tf_op jit(solution)/shard_map/outer/pallas_call | solution.py:242
  46.6 11.0 %all_to_all.10 = f16[16,3,8,128]{3,2,1,0:T(8,128)(2,1)S(1)} all-to-all(f16[16,3,8,128]{3,2,1,0:T(8,128)(2,1)S(1)} %convert_element_type.50), channel_id=1, replica_groups=mesh['chip'=16,'core'=2,'zl'=2,'y'=8] {'zl','y'}, dimensions={0} | all-to-all | bytes 196608 | tf_op jit(solution)/shard_map/all_to_all | solution.py:253
  57.5 0.7 %copy_bitcast_fusion = f32[3,8,2048]{2,1,0:T(8,128)} fusion(f16[16,3,8,128]{3,2,1,0:T(8,128)(2,1)S(1)} %all_to_all.10), kind=kLoop, calls=%fused_computation | loop fusion | flops 98304 | bytes 294912 | tf_op jit(solution)/shard_map/mul | solution.py:254
  (10 shorter events, 0.2 us)
Async XLA Ops:
  1.6 17.1 %all-to-all-start = ((f16[3,8,16,128]{3,1,0,2:T(8,128)(2,1)}), f16[3,8,16,128]{3,1,0,2:T(8,128)(2,1)S(1)}, u32[]{:S(2)}, u32[]{:S(2)}) async-start(f16[3,8,16,128]{3,1,0,2:T(8,128)(2,1)} %copy_bitcast_fusion.1), calls=%async_computation | async-start | bytes 196608 | tf_op jit(solution)/shard_map/all_to_all | solution.py:215

commit v7 on v6

--- a/solution.py
+++ b/solution.py
@@ -217,7 +217,7 @@
     high = speed.astype(F16)
     rest = ((speed - high.astype(F32)) * 2048.0).astype(F16)
     own = blocks.transpose(0, 2, 1, 3).reshape(3, K, CELLS)
-    own = jnp.concatenate([own, high[:, None], rest[:, None], jnp.zeros((3, 14, CELLS), F16)], axis=1)
+    own = jnp.concatenate([own, high[:, None], rest[:, None], jnp.zeros((3, 6, CELLS), F16)], axis=1)
     chip = lax.all_gather(own, "core", axis=0, tiled=True)
     place = jnp.stack([core, jnp.where(lax.axis_index("chip") % 4 < 2, 0, 1).astype(jnp.int32)])
     wide = chip.astype(F32)

time: 58.6 us -> 58.4 us (level)
  no operation moved by 1% of the time
where the time goes in v7:
time: 58.4 us; the launch traced here: 58 us
  blocking collectives  26.5 us (45%)
  Pallas kernels  12.8 us (22%)
  starting transfers between devices  9.56 us (16%)
  other arithmetic  4.94 us (8%)
  waiting for transfers between devices  3.92 us (7%)
    all_to_all x1, blocking collectives, on_device(): lax.all_to_all(blocks.astype(F16), SECT, split_axis=0, concat_axis=0, til...  10.9 us
    all_to_all x1, starting transfers between devices, on_device(): lax.all_to_all(blocks, SECT, split_axis=2, concat_axis=2, tiled=True)  9.56 us
    all_gather x1, blocking collectives, on_device(): far = lax.all_gather(edge, SPACE, axis=0, axis_index_groups=neighbours)  9.37 us
    pallas_call x1, Pallas kernels, on_device(): pl.pallas_call(outer_kernel, out_shape=[jax.ShapeDtypeStruct((16, 3, 8, C...  6.03 us
    pallas_call x1, Pallas kernels, on_device(): pl.pallas_call(before_kernel, out_shape=shapes, in_specs=[SMEM] + [VMEM]...  5.87 us
    all_to_all x1, waiting for transfers between devices, on_device(): lax.all_to_all(blocks, SECT, split_axis=2, concat_axis=2, tiled=True)  3.92 us
    all_gather x1, blocking collectives, on_device(): chip = lax.all_gather(own, 'core', axis=0, tiled=True)  3.61 us
    all_gather x1, blocking collectives, on_device(): lax.all_gather(lax.dynamic_index_in_dim(far, 3 * (1 - core), 0, keepdims=...  2.62 us
  transfers between devices with their start and end apart: 1, of which 1 were waited for; matrix products, arithmetic and copies ran while one was open for 4% of the time, Pallas kernels for 2%

profile of v7, /device:TPU:1, one launch (start us, length us, event | category | flops | bytes accessed | tf_op | source)
XLA Modules:
  0.0 58.0 jit_solution(5000755879521224619)
XLA Ops:
  0.0 1.6 %copy_bitcast_fusion.1 = f16[3,8,16,128]{3,1,0,2:T(8,128)(2,1)} fusion(f32[3,8,2048]{2,1,0:T(8,128)} %param.5), kind=kLoop, calls=%fused_computation.5 | loop fusion | flops 49152 | bytes 294912 | tf_op jit(solution)/shard_map/convert_element_type | solution.py:214
  1.6 9.6 %all-to-all-start = ((f16[3,8,16,128]{3,1,0,2:T(8,128)(2,1)}), f16[3,8,16,128]{3,1,0,2:T(8,128)(2,1)S(1)}, u32[]{:S(2)}, u32[]{:S(2)}) async-start(f16[3,8,16,128]{3,1,0,2:T(8,128)(2,1)} %copy_bitcast_fusion.1), calls=%async_computation | async-start | bytes 196608 | tf_op jit(solution)/shard_map/all_to_all | solution.py:215
  11.2 0.7 %fusion.1 = (f16[3,1,128]{2,0,1:T(4,128)(2,1)S(1)}, f16[3,1,128]{2,0,1:T(4,128)(2,1)S(1)}) fusion(f32[3,2048]{1,0:T(4,128)} %param.6, s32[]{:T(128)S(6)} %select_n.35), kind=kLoop, calls=%fused_computation.15 | loop fusion | flops 1920 | bytes 3076 | tf_op jit(solution)/shard_map/broadcast_in_dim | solution.py:220
  11.9 0.8 %convert_element_type.45 = f32[128,128]{1,0:T(8,128)S(1)} convert(s32[128,128]{1,0:T(8,128)} %param.9) | non-fusion elementwise | flops 16384 | bytes 131072 | tf_op jit(solution)/shard_map/convert_element_type | solution.py:80
  12.7 0.9 %pad_maximum_fusion.table_ref = f32[384,128]{1,0:T(8,128)S(1)} fusion(f32[128,128]{1,0:T(8,128)S(1)} %convert_element_type.45, f32[128,128]{1,0:T(8,128)} %param.8, f32[128,128]{1,0:T(8,128)} %param.7), kind=kLoop, calls=%fused_computation.1 | loop fusion | flops 98304 | bytes 393216 | tf_op jit(solution)/shard_map/concatenate | solution.py:80
  13.6 0.9 %prepare.1 = (bf16[128,128]{1,0:T(8,128)(2,1)S(1)}, bf16[128,9216]{1,0:T(8,128)(2,1)S(1)}) custom-call(f32[384,128]{1,0:T(8,128)S(1)} %pad_maximum_fusion.table_ref), custom_call_target="tpu_custom_call" | custom-call | tf_op jit(solution)/shard_map/prepare/pallas_call | solution.py:73
  14.6 0.1 pad.6.clone
  14.7 0.1 pad_add_fusion.place_ref
  14.7 3.9 %all-to-all-done = f16[3,8,16,128]{3,1,0,2:T(8,128)(2,1)S(1)} async-done(((f16[3,8,16,128]{3,1,0,2:T(8,128)(2,1)}), f16[3,8,16,128]{3,1,0,2:T(8,128)(2,1)S(1)}, u32[]{:S(2)}, u32[]{:S(2)}) %all-to-all-start) | async-done | bytes 98336 | tf_op jit(solution)/shard_map/all_to_all | solution.py:215
  18.7 0.1 maximum_maximum_fusion
  18.8 3.6 %all_gather.13 = f16[6,136,128]{2,1,0:T(8,128)(2,1)S(1)} all-gather(f16[3,136,128]{2,1,0:T(8,128)(2,1)S(1)} %maximum_maximum_fusion), channel_id=1, replica_groups=mesh['chip'=16,'core'=2,'zl'=2,'y'=8] {'core'}, dimensions={0}, use_global_device_ids=true | all-gather | bytes 313344 | tf_op jit(solution)/shard_map/all_gather | solution.py:221
  22.5 5.9 %before.1 = (f32[2,128,128]{2,1,0:T(8,128)S(1)}, f32[4,128,128]{2,1,0:T(8,128)S(1)}, f32[2,128,128]{2,1,0:T(8,128)S(1)}, f32[2,128,128]{2,1,0:T(8,128)S(1)}, f32[2,128,128]{2,1,0:T(8,128)S(1)}) custom-call(s32[2]{0:T(128)S(1)} %pad_add_fusion.place_ref, f32[6,136,128]{2,1,0:T(8,128)S(1)} %convert_element_type.44.chip_ref, ...), custom_call_target="tpu_custom_call" | custom-call | flops 3623878656 | bytes 3000000 | tf_op jit(solution)/shard_map/before/pallas_call | solution.py:225
  28.3 9.4 %all-gather = f16[8,136,128]{2,1,0:T(8,128)(2,1)S(1)} all-gather(f16[4,136,128]{2,1,0:T(8,128)(2,1)S(1)} %constant_dynamic-slice_fusion.1), channel_id=2, replica_groups={{16,32},{48,64},{80,96},{112,128},{144,160},{176,192},{208,224},{240,25..., dimensions={0}, use_global_device_ids=true | all-gather | bytes 417792 | tf_op jit(solution)/shard_map/all_gather | solution.py:238
  37.8 2.6 %all-gather.1 = f16[2,1,136,128]{3,2,1,0:T(8,128)(2,1)S(1)} all-gather(f16[1,1,136,128]{3,2,1,0:T(8,128)(2,1)S(1)} %constant_dynamic-slice_fusion), channel_id=3, replica_groups=mesh['chip'=16,'core'=2,'zl'=2,'y'=8] {'core'}, dimensions={0}, use_global_device_ids=true | all-gather | bytes 104448 | tf_op jit(solution)/shard_map/all_gather | solution.py:240
  40.4 6.0 %outer.1 = (f32[16,3,8,128]{3,2,1,0:T(8,128)S(1)}, f32[2,128,128]{2,1,0:T(8,128)S(1)}, f32[4,128,128]{2,1,0:T(8,128)S(1)}, f32[2,128,128]{2,1,0:T(8,128)S(1)}, f...) custom-call(s32[2]{0:T(128)S(1)} %pad_add_fusion.place_ref, ...), custom_call_target="tpu_custom_call", output_to_operand_aliasing={{1}: (6, {}), {2}: (7, {}), {3}: (8, {}), {4}: (9, {}), {5}... | custom-call | flops 3623878656 | bytes 3000000 | tf_op jit(solution)/shard_map/outer/pallas_call | solution.py:242
  46.5 10.9 %all_to_all.10 = f16[16,3,8,128]{3,2,1,0:T(8,128)(2,1)S(1)} all-to-all(f16[16,3,8,128]{3,2,1,0:T(8,128)(2,1)S(1)} %convert_element_type.50), channel_id=1, replica_groups=mesh['chip'=16,'core'=2,'zl'=2,'y'=8] {'zl','y'}, dimensions={0} | all-to-all | bytes 196608 | tf_op jit(solution)/shard_map/all_to_all | solution.py:253
  57.3 0.7 %copy_bitcast_fusion = f32[3,8,2048]{2,1,0:T(8,128)} fusion(f16[16,3,8,128]{3,2,1,0:T(8,128)(2,1)S(1)} %all_to_all.10), kind=kLoop, calls=%fused_computation | loop fusion | flops 98304 | bytes 294912 | tf_op jit(solution)/shard_map/mul | solution.py:254
  (10 shorter events, 0.2 us)
Async XLA Ops:
  1.6 17.1 %all-to-all-start = ((f16[3,8,16,128]{3,1,0,2:T(8,128)(2,1)}), f16[3,8,16,128]{3,1,0,2:T(8,128)(2,1)S(1)}, u32[]{:S(2)}, u32[]{:S(2)}) async-start(f16[3,8,16,128]{3,1,0,2:T(8,128)(2,1)} %copy_bitcast_fusion.1), calls=%async_computation | async-start | bytes 196608 | tf_op jit(solution)/shard_map/all_to_all | solution.py:215

commit v8 on v7

--- a/solution.py
+++ b/solution.py
@@ -233,10 +233,12 @@
         name="before",
     )(place, wide, beta, coef)
     edge = lax.dynamic_slice_in_dim(chip, 2 * core, 4, 0)
+    edge = jnp.concatenate([edge[:, :K].reshape(4 * K, CELLS), edge[:, K : K + 2].reshape(8, CELLS)])
     edge, found = lax.optimization_barrier((edge, found))
     neighbours = [[s, (s + 1) % 32] for s in range(1, 32, 2)]
     far = lax.all_gather(edge, SPACE, axis=0, axis_index_groups=neighbours)
     far = lax.dynamic_index_in_dim(far, core, 0, keepdims=False)
+    far = jnp.concatenate([far[: 4 * K].reshape(4, K, CELLS), far[4 * K :].reshape(4, 2, CELLS)], axis=1)
     near = lax.all_gather(lax.dynamic_index_in_dim(far, 3 * (1 - core), 0, keepdims=False), "core", axis=0)
     near = lax.dynamic_index_in_dim(near, 1 - core, 0, keepdims=False)
     blocks, *_ = pl.pallas_call(

time: 58.4 us -> 58.4 us (level)
  no operation moved by 1% of the time
where the time goes in v8:
time: 58.4 us; the launch traced here: 58 us
  blocking collectives  26.4 us (45%)
  Pallas kernels  12.8 us (22%)
  starting transfers between devices  9.56 us (16%)
  other arithmetic  5.01 us (9%)
  waiting for transfers between devices  3.93 us (7%)
    all_to_all x1, blocking collectives, on_device(): lax.all_to_all(blocks.astype(F16), SECT, split_axis=0, concat_axis=0, til...  10.8 us
    all_to_all x1, starting transfers between devices, on_device(): lax.all_to_all(blocks, SECT, split_axis=2, concat_axis=2, tiled=True)  9.56 us
    all_gather x1, blocking collectives, on_device(): far = lax.all_gather(edge, SPACE, axis=0, axis_index_groups=neighbours)  9.25 us
    pallas_call x1, Pallas kernels, on_device(): pl.pallas_call(outer_kernel, out_shape=[jax.ShapeDtypeStruct((16, 3, 8, C...  6.03 us
    pallas_call x1, Pallas kernels, on_device(): pl.pallas_call(before_kernel, out_shape=shapes, in_specs=[SMEM] + [VMEM]...  5.87 us
    all_to_all x1, waiting for transfers between devices, on_device(): lax.all_to_all(blocks, SECT, split_axis=2, concat_axis=2, tiled=True)  3.93 us
    all_gather x1, blocking collectives, on_device(): chip = lax.all_gather(own, 'core', axis=0, tiled=True)  3.61 us
    all_gather x1, blocking collectives, on_device(): lax.all_gather(lax.dynamic_index_in_dim(far, 3 * (1 - core), 0, keepdims=...  2.68 us
  transfers between devices with their start and end apart: 1, of which 1 were waited for; matrix products, arithmetic and copies ran while one was open for 4% of the time, Pallas kernels for 2%

profile of v8, /device:TPU:1, one launch (start us, length us, event | category | flops | bytes accessed | tf_op | source)
XLA Modules:
  0.0 58.0 jit_solution(5986606989176762591)
XLA Ops:
  0.0 1.6 %copy_bitcast_fusion.1 = f16[3,8,16,128]{3,1,0,2:T(8,128)(2,1)} fusion(f32[3,8,2048]{2,1,0:T(8,128)} %param.5), kind=kLoop, calls=%fused_computation.9 | loop fusion | flops 49152 | bytes 294912 | tf_op jit(solution)/shard_map/convert_element_type | solution.py:214
  1.6 9.6 %all-to-all-start = ((f16[3,8,16,128]{3,1,0,2:T(8,128)(2,1)}), f16[3,8,16,128]{3,1,0,2:T(8,128)(2,1)S(1)}, u32[]{:S(2)}, u32[]{:S(2)}) async-start(f16[3,8,16,128]{3,1,0,2:T(8,128)(2,1)} %copy_bitcast_fusion.1), calls=%async_computation | async-start | bytes 196608 | tf_op jit(solution)/shard_map/all_to_all | solution.py:215
  11.2 0.7 %fusion.4 = (f16[3,1,128]{2,0,1:T(4,128)(2,1)S(1)}, f16[3,1,128]{2,0,1:T(4,128)(2,1)S(1)}) fusion(f32[3,2048]{1,0:T(4,128)} %param.6, s32[]{:T(128)S(6)} %select_n.31), kind=kLoop, calls=%fused_computation.23 | loop fusion | flops 1920 | bytes 3076 | tf_op jit(solution)/shard_map/broadcast_in_dim | solution.py:220
  11.9 0.8 %convert_element_type.43 = f32[128,128]{1,0:T(8,128)S(1)} convert(s32[128,128]{1,0:T(8,128)} %param.9) | non-fusion elementwise | flops 16384 | bytes 131072 | tf_op jit(solution)/shard_map/convert_element_type | solution.py:80
  12.7 0.9 %pad_maximum_fusion.table_ref = f32[384,128]{1,0:T(8,128)S(1)} fusion(f32[128,128]{1,0:T(8,128)S(1)} %convert_element_type.43, f32[128,128]{1,0:T(8,128)} %param.8, f32[128,128]{1,0:T(8,128)} %param.7), kind=kLoop, calls=%fused_computation.1 | loop fusion | flops 98304 | bytes 393216 | tf_op jit(solution)/shard_map/concatenate | solution.py:80
  13.6 0.9 %prepare.1 = (bf16[128,128]{1,0:T(8,128)(2,1)S(1)}, bf16[128,9216]{1,0:T(8,128)(2,1)S(1)}) custom-call(f32[384,128]{1,0:T(8,128)S(1)} %pad_maximum_fusion.table_ref), custom_call_target="tpu_custom_call" | custom-call | tf_op jit(solution)/shard_map/prepare/pallas_call | solution.py:73
  14.6 0.1 pad.10.clone
  14.6 0.1 pad_add_fusion.place_ref
  14.7 3.9 %all-to-all-done = f16[3,8,16,128]{3,1,0,2:T(8,128)(2,1)S(1)} async-done(((f16[3,8,16,128]{3,1,0,2:T(8,128)(2,1)}), f16[3,8,16,128]{3,1,0,2:T(8,128)(2,1)S(1)}, u32[]{:S(2)}, u32[]{:S(2)}) %all-to-all-start) | async-done | bytes 98336 | tf_op jit(solution)/shard_map/all_to_all | solution.py:215
  18.7 0.1 maximum_maximum_fusion
  18.8 3.6 %all_gather.13 = f16[6,136,128]{2,1,0:T(8,128)(2,1)S(1)} all-gather(f16[3,136,128]{2,1,0:T(8,128)(2,1)S(1)} %maximum_maximum_fusion), channel_id=1, replica_groups=mesh['chip'=16,'core'=2,'zl'=2,'y'=8] {'core'}, dimensions={0}, use_global_device_ids=true | all-gather | bytes 313344 | tf_op jit(solution)/shard_map/all_gather | solution.py:221
  22.5 5.9 %before.1 = (f32[2,128,128]{2,1,0:T(8,128)S(1)}, f32[4,128,128]{2,1,0:T(8,128)S(1)}, f32[2,128,128]{2,1,0:T(8,128)S(1)}, f32[2,128,128]{2,1,0:T(8,128)S(1)}, f32[2,128,128]{2,1,0:T(8,128)S(1)}) custom-call(s32[2]{0:T(128)S(1)} %pad_add_fusion.place_ref, f32[6,136,128]{2,1,0:T(8,128)S(1)} %convert_element_type.42.chip_ref, ...), custom_call_target="tpu_custom_call" | custom-call | flops 3623878656 | bytes 3000000 | tf_op jit(solution)/shard_map/before/pallas_call | solution.py:225
  28.4 9.2 %all-gather = f16[1040,128]{1,0:T(8,128)(2,1)S(1)} all-gather(f16[520,128]{1,0:T(8,128)(2,1)S(1)} %pad_maximum_fusion.2), channel_id=2, replica_groups={{16,32},{48,64},{80,96},{112,128},{144,160},{176,192},{208,224},{240,25..., dimensions={0}, use_global_device_ids=true | all-gather | bytes 399360 | tf_op jit(solution)/shard_map/all_gather | solution.py:239
  37.8 2.7 %all_gather.16 = f16[2,130,128]{2,1,0:T(8,128)(2,1)S(1)} all-gather(f16[1,130,128]{2,1,0:T(8,128)(2,1)S(1)} %fusion.1), channel_id=1, replica_groups=mesh['chip'=16,'core'=2,'zl'=2,'y'=8] {'core'}, dimensions={0}, use_global_device_ids=true | all-gather | bytes 99840 | tf_op jit(solution)/shard_map/all_gather | solution.py:242
  40.5 6.0 %outer.1 = (f32[16,3,8,128]{3,2,1,0:T(8,128)S(1)}, f32[2,128,128]{2,1,0:T(8,128)S(1)}, f32[4,128,128]{2,1,0:T(8,128)S(1)}, f32[2,128,128]{2,1,0:T(8,128)S(1)}, f...) custom-call(s32[2]{0:T(128)S(1)} %pad_add_fusion.place_ref, ...), custom_call_target="tpu_custom_call", output_to_operand_aliasing={{1}: (6, {}), {2}: (7, {}), {3}: (8, {}), {4}: (9, {}), {5}... | custom-call | flops 3623878656 | bytes 3000000 | tf_op jit(solution)/shard_map/outer/pallas_call | solution.py:244
  46.5 10.8 %all_to_all.10 = f16[16,3,8,128]{3,2,1,0:T(8,128)(2,1)S(1)} all-to-all(f16[16,3,8,128]{3,2,1,0:T(8,128)(2,1)S(1)} %convert_element_type.47), channel_id=1, replica_groups=mesh['chip'=16,'core'=2,'zl'=2,'y'=8] {'zl','y'}, dimensions={0} | all-to-all | bytes 196608 | tf_op jit(solution)/shard_map/all_to_all | solution.py:255
  57.3 0.7 %copy_bitcast_fusion = f32[3,8,2048]{2,1,0:T(8,128)} fusion(f16[16,3,8,128]{3,2,1,0:T(8,128)(2,1)S(1)} %all_to_all.10), kind=kLoop, calls=%fused_computation | loop fusion | flops 98304 | bytes 294912 | tf_op jit(solution)/shard_map/mul | solution.py:256
  (14 shorter events, 0.3 us)
Async XLA Ops:
  1.6 17.1 %all-to-all-start = ((f16[3,8,16,128]{3,1,0,2:T(8,128)(2,1)}), f16[3,8,16,128]{3,1,0,2:T(8,128)(2,1)S(1)}, u32[]{:S(2)}, u32[]{:S(2)}) async-start(f16[3,8,16,128]{3,1,0,2:T(8,128)(2,1)} %copy_bitcast_fusion.1), calls=%async_computation | async-start | bytes 196608 | tf_op jit(solution)/shard_map/all_to_all | solution.py:215

commit v9 on v7

--- a/solution.py
+++ b/solution.py
@@ -219,7 +219,7 @@
     own = blocks.transpose(0, 2, 1, 3).reshape(3, K, CELLS)
     own = jnp.concatenate([own, high[:, None], rest[:, None], jnp.zeros((3, 6, CELLS), F16)], axis=1)
     chip = lax.all_gather(own, "core", axis=0, tiled=True)
-    place = jnp.stack([core, jnp.where(lax.axis_index("chip") % 4 < 2, 0, 1).astype(jnp.int32)])
+    place = jnp.stack([core, jnp.where(lax.axis_index("chip") % 4 < 1, 0, 1).astype(jnp.int32)])
     wide = chip.astype(F32)
     shapes = [jax.ShapeDtypeStruct((n, K, CELLS), F32) for n in (2, 4, 2, 2, 2)]
     found = pl.pallas_call(

time: 58.4 us -> 58.2 us (level)
    all_gather x1, blocking collectives: 2.62 us -> 4.89 us  [on_device(): lax.all_gather(lax.dynamic_index_in_dim(far, 3 * (1 - core), 0, keepdims=...]
    all_gather x1, blocking collectives: 9.37 us -> 7.85 us  [on_device(): far = lax.all_gather(edge, SPACE, axis=0, axis_index_groups=neighbours)]
    all_to_all x1, blocking collectives: 10.9 us -> 9.98 us  [on_device(): lax.all_to_all(blocks.astype(F16), SECT, split_axis=0, concat_axis=0, til...]
where the time goes in v9:
time: 58.2 us; the launch traced here: 57.9 us
  blocking collectives  26.3 us (45%)
  Pallas kernels  12.8 us (22%)
  starting transfers between devices  9.56 us (16%)
  other arithmetic  4.94 us (8%)
  waiting for transfers between devices  3.92 us (7%)
    all_to_all x1, blocking collectives, on_device(): lax.all_to_all(blocks.astype(F16), SECT, split_axis=0, concat_axis=0, til...  9.98 us
    all_to_all x1, starting transfers between devices, on_device(): lax.all_to_all(blocks, SECT, split_axis=2, concat_axis=2, tiled=True)  9.56 us
    all_gather x1, blocking collectives, on_device(): far = lax.all_gather(edge, SPACE, axis=0, axis_index_groups=neighbours)  7.85 us
    pallas_call x1, Pallas kernels, on_device(): pl.pallas_call(outer_kernel, out_shape=[jax.ShapeDtypeStruct((16, 3, 8, C...  6.02 us
    pallas_call x1, Pallas kernels, on_device(): pl.pallas_call(before_kernel, out_shape=shapes, in_specs=[SMEM] + [VMEM]...  5.87 us
    all_gather x1, blocking collectives, on_device(): lax.all_gather(lax.dynamic_index_in_dim(far, 3 * (1 - core), 0, keepdims=...  4.89 us
    all_to_all x1, waiting for transfers between devices, on_device(): lax.all_to_all(blocks, SECT, split_axis=2, concat_axis=2, tiled=True)  3.92 us
    all_gather x1, blocking collectives, on_device(): chip = lax.all_gather(own, 'core', axis=0, tiled=True)  3.61 us
  transfers between devices with their start and end apart: 1, of which 1 were waited for; matrix products, arithmetic and copies ran while one was open for 4% of the time, Pallas kernels for 2%

profile of v9, /device:TPU:1, one launch (start us, length us, event | category | flops | bytes accessed | tf_op | source)
XLA Modules:
  0.0 57.9 jit_solution(9691699225255866605)
XLA Ops:
  0.0 1.6 %copy_bitcast_fusion.1 = f16[3,8,16,128]{3,1,0,2:T(8,128)(2,1)} fusion(f32[3,8,2048]{2,1,0:T(8,128)} %param.5), kind=kLoop, calls=%fused_computation.5 | loop fusion | flops 49152 | bytes 294912 | tf_op jit(solution)/shard_map/convert_element_type | solution.py:214
  1.6 9.6 %all-to-all-start = ((f16[3,8,16,128]{3,1,0,2:T(8,128)(2,1)}), f16[3,8,16,128]{3,1,0,2:T(8,128)(2,1)S(1)}, u32[]{:S(2)}, u32[]{:S(2)}) async-start(f16[3,8,16,128]{3,1,0,2:T(8,128)(2,1)} %copy_bitcast_fusion.1), calls=%async_computation | async-start | bytes 196608 | tf_op jit(solution)/shard_map/all_to_all | solution.py:215
  11.2 0.7 %fusion.1 = (f16[3,1,128]{2,0,1:T(4,128)(2,1)S(1)}, f16[3,1,128]{2,0,1:T(4,128)(2,1)S(1)}) fusion(f32[3,2048]{1,0:T(4,128)} %param.6, s32[]{:T(128)S(6)} %select_n.35), kind=kLoop, calls=%fused_computation.15 | loop fusion | flops 1920 | bytes 3076 | tf_op jit(solution)/shard_map/broadcast_in_dim | solution.py:220
  11.9 0.8 %convert_element_type.45 = f32[128,128]{1,0:T(8,128)S(1)} convert(s32[128,128]{1,0:T(8,128)} %param.9) | non-fusion elementwise | flops 16384 | bytes 131072 | tf_op jit(solution)/shard_map/convert_element_type | solution.py:80
  12.7 0.9 %pad_maximum_fusion.table_ref = f32[384,128]{1,0:T(8,128)S(1)} fusion(f32[128,128]{1,0:T(8,128)S(1)} %convert_element_type.45, f32[128,128]{1,0:T(8,128)} %param.8, f32[128,128]{1,0:T(8,128)} %param.7), kind=kLoop, calls=%fused_computation.1 | loop fusion | flops 98304 | bytes 393216 | tf_op jit(solution)/shard_map/concatenate | solution.py:80
  13.6 0.9 %prepare.1 = (bf16[128,128]{1,0:T(8,128)(2,1)S(1)}, bf16[128,9216]{1,0:T(8,128)(2,1)S(1)}) custom-call(f32[384,128]{1,0:T(8,128)S(1)} %pad_maximum_fusion.table_ref), custom_call_target="tpu_custom_call" | custom-call | tf_op jit(solution)/shard_map/prepare/pallas_call | solution.py:73
  14.6 0.1 pad.6.clone
  14.7 0.1 pad_add_fusion.place_ref
  14.7 3.9 %all-to-all-done = f16[3,8,16,128]{3,1,0,2:T(8,128)(2,1)S(1)} async-done(((f16[3,8,16,128]{3,1,0,2:T(8,128)(2,1)}), f16[3,8,16,128]{3,1,0,2:T(8,128)(2,1)S(1)}, u32[]{:S(2)}, u32[]{:S(2)}) %all-to-all-start) | async-done | bytes 98336 | tf_op jit(solution)/shard_map/all_to_all | solution.py:215
  18.7 0.1 maximum_maximum_fusion
  18.8 3.6 %all_gather.13 = f16[6,136,128]{2,1,0:T(8,128)(2,1)S(1)} all-gather(f16[3,136,128]{2,1,0:T(8,128)(2,1)S(1)} %maximum_maximum_fusion), channel_id=1, replica_groups=mesh['chip'=16,'core'=2,'zl'=2,'y'=8] {'core'}, dimensions={0}, use_global_device_ids=true | all-gather | bytes 313344 | tf_op jit(solution)/shard_map/all_gather | solution.py:221
  22.5 5.9 %before.1 = (f32[2,128,128]{2,1,0:T(8,128)S(1)}, f32[4,128,128]{2,1,0:T(8,128)S(1)}, f32[2,128,128]{2,1,0:T(8,128)S(1)}, f32[2,128,128]{2,1,0:T(8,128)S(1)}, f32[2,128,128]{2,1,0:T(8,128)S(1)}) custom-call(s32[2]{0:T(128)S(1)} %pad_add_fusion.place_ref, f32[6,136,128]{2,1,0:T(8,128)S(1)} %convert_element_type.44.chip_ref, ...), custom_call_target="tpu_custom_call" | custom-call | flops 3623878656 | bytes 3000000 | tf_op jit(solution)/shard_map/before/pallas_call | solution.py:225
  28.3 7.8 %all-gather = f16[8,136,128]{2,1,0:T(8,128)(2,1)S(1)} all-gather(f16[4,136,128]{2,1,0:T(8,128)(2,1)S(1)} %constant_dynamic-slice_fusion.1), channel_id=2, replica_groups={{16,32},{48,64},{80,96},{112,128},{144,160},{176,192},{208,224},{240,25..., dimensions={0}, use_global_device_ids=true | all-gather | bytes 417792 | tf_op jit(solution)/shard_map/all_gather | solution.py:238
  36.2 4.9 %all-gather.1 = f16[2,1,136,128]{3,2,1,0:T(8,128)(2,1)S(1)} all-gather(f16[1,1,136,128]{3,2,1,0:T(8,128)(2,1)S(1)} %constant_dynamic-slice_fusion), channel_id=3, replica_groups=mesh['chip'=16,'core'=2,'zl'=2,'y'=8] {'core'}, dimensions={0}, use_global_device_ids=true | all-gather | bytes 104448 | tf_op jit(solution)/shard_map/all_gather | solution.py:240
  41.1 6.0 %outer.1 = (f32[16,3,8,128]{3,2,1,0:T(8,128)S(1)}, f32[2,128,128]{2,1,0:T(8,128)S(1)}, f32[4,128,128]{2,1,0:T(8,128)S(1)}, f32[2,128,128]{2,1,0:T(8,128)S(1)}, f...) custom-call(s32[2]{0:T(128)S(1)} %pad_add_fusion.place_ref, ...), custom_call_target="tpu_custom_call", output_to_operand_aliasing={{1}: (6, {}), {2}: (7, {}), {3}: (8, {}), {4}: (9, {}), {5}... | custom-call | flops 3623878656 | bytes 3000000 | tf_op jit(solution)/shard_map/outer/pallas_call | solution.py:242
  47.2 10.0 %all_to_all.10 = f16[16,3,8,128]{3,2,1,0:T(8,128)(2,1)S(1)} all-to-all(f16[16,3,8,128]{3,2,1,0:T(8,128)(2,1)S(1)} %convert_element_type.50), channel_id=1, replica_groups=mesh['chip'=16,'core'=2,'zl'=2,'y'=8] {'zl','y'}, dimensions={0} | all-to-all | bytes 196608 | tf_op jit(solution)/shard_map/all_to_all | solution.py:253
  57.2 0.7 %copy_bitcast_fusion = f32[3,8,2048]{2,1,0:T(8,128)} fusion(f16[16,3,8,128]{3,2,1,0:T(8,128)(2,1)S(1)} %all_to_all.10), kind=kLoop, calls=%fused_computation | loop fusion | flops 98304 | bytes 294912 | tf_op jit(solution)/shard_map/mul | solution.py:254
  (10 shorter events, 0.2 us)
Async XLA Ops:
  1.6 17.1 %all-to-all-start = ((f16[3,8,16,128]{3,1,0,2:T(8,128)(2,1)}), f16[3,8,16,128]{3,1,0,2:T(8,128)(2,1)S(1)}, u32[]{:S(2)}, u32[]{:S(2)}) async-start(f16[3,8,16,128]{3,1,0,2:T(8,128)(2,1)} %copy_bitcast_fusion.1), calls=%async_computation | async-start | bytes 196608 | tf_op jit(solution)/shard_map/all_to_all | solution.py:215
